TPU v7x, 32 devices: a whole 2x2x4 slice. The times are simulated.
32 devices in a mesh: dp: 8 (over z, y), shard: 4 (over x, core).
Axes of the slice: x: 2, y: 2, z: 4, core: 2. Of those that a mesh axis runs over, the one named last changes fastest.
Arguments:
- tokens: float32 [36864, 768], P(('dp', 'shard')), may hold values from -6 to 6
- cotangent: float32 [36864, 768], P(('dp', 'shard')), may hold values from -6 to 6
- lengths: int32 [128], P(('dp', 'shard')), may hold values from 64 to 288, as said below
- null_flags: int32 [128], P(('dp', 'shard')), may hold values 0 or 1
- weights: float32 [768, 9216], P(('dp', 'shard')), as said below
- moment1: float32 [768, 9216], P(('dp', 'shard')), as said below
- moment2: float32 [768, 9216], P(('dp', 'shard')), as said below
- vectors: float32 [12, 768], replicated, as said below
- vec_moment1: float32 [12, 768], replicated, as said below
- vec_moment2: float32 [12, 768], replicated, as said below
Outputs:
- output: float32 [36864, 768], P(('dp', 'shard'))
- input_grad: float32 [36864, 768], P(('dp', 'shard'))
- new_moment1: float32 [768, 9216], P(('dp', 'shard'))
- new_moment2: float32 [768, 9216], P(('dp', 'shard'))
- new_weights: float32 [768, 9216], P(('dp', 'shard'))
- new_vec_moment1: float32 [12, 768], replicated
- new_vec_moment2: float32 [12, 768], replicated
- new_vectors: float32 [12, 768], replicated
- norm_pairs: float32 [4, 2], replicated
- trust: float32 [4], replicated
Inputs may be any that keep to these rules, and one draw needn't show every extreme that they name: `lengths`: valid tokens of a slot, its query included. `null_flags`: 1 marks a null document, of which only the first 64 tokens count. float32 master weights. `moment1`: first moments. `moment2`: positive second moments. `vectors`: gains near one, small biases. `vec_moment1`: first moments. `vec_moment2`: positive second moments.
All inputs are finite; a program needn't handle non-finite values. No bound on the sum of `null_flags` on one device may be relied on, other than what follows from the above.
Results may differ from a plain program's by a relative error of at most 0.013.
The roundings to bfloat16 on the way count: a program that leaves them out, or rounds other values in their place, can miss the bound.
Values may be sent and summed in bfloat16 or wider, within the bound.
A program may use at most 192 MiB of HBM per device.

v0:
```python
import jax
import jax.numpy as jnp
from jax import lax
from jax.sharding import PartitionSpec as P

HEADS = 12
SLOT = 288
QLEN = 64
STEP = 5


def norm_forward(values, gain, shift):
    centred = values - jnp.mean(values, axis=-1, keepdims=True)
    inverse = lax.rsqrt(jnp.mean(centred * centred, axis=-1, keepdims=True) + 1e-05)
    normed = centred * inverse
    return (normed * gain + shift, normed, inverse)


def norm_backward(grad_result, normed, inverse, gain):
    scaled = grad_result * gain
    grad_gain = jnp.sum(grad_result * normed, axis=0)
    grad_shift = jnp.sum(grad_result, axis=0)
    centred = scaled - jnp.mean(scaled, axis=-1, keepdims=True)
    grad_input = inverse * (centred - normed * jnp.mean(scaled * normed, axis=-1, keepdims=True))
    return (grad_input, grad_gain, grad_shift)


def gelu_slope(values):
    return (
        0.5 * (1.0 + jax.scipy.special.erf(values * 0.7071067811865476))
        + values * jnp.exp(-0.5 * values * values) * 0.3989422804014327
    )


def local(
    tokens,
    cotangent,
    lengths,
    null_flags,
    weights,
    moment1,
    moment2,
    vectors,
    vec_moment1,
    vec_moment2,
):
    model_width = tokens.shape[1]
    row_count = tokens.shape[0]
    slot_count = lengths.shape[0]
    head_size = model_width // HEADS
    score_scale = head_size ** (-0.5)
    block_slots = min(2, slot_count)
    block_count = slot_count // block_slots
    valid_len = jnp.where(null_flags == 1, QLEN, lengths)
    key_valid = jnp.arange(SLOT, dtype=jnp.int32)[None, :] < valid_len[:, None]
    key_blocks = key_valid.reshape(block_count, block_slots, SLOT)
    row_weight = key_valid.reshape(row_count, 1).astype(jnp.float32)
    qkv_bias = jnp.concatenate([vectors[0], jnp.zeros((model_width,), jnp.float32), vectors[1]])
    ffn_bias = vectors[8:12].reshape(4 * model_width)
    token_low = tokens.astype(jnp.bfloat16)

    def block_scores(qkv_block, valid_keys):
        scores = (
            jnp.einsum(
                "bqhd,bkhd->bhqk",
                qkv_block[:, :, 0],
                qkv_block[:, :, 1],
                preferred_element_type=jnp.float32,
            )
            * score_scale
        )
        return jnp.where(valid_keys[:, None, None, :], scores, -1000000000.0)

    def attend_block(packed):
        qkv_block, valid_keys = packed
        scores = block_scores(qkv_block, valid_keys)
        row_top = jnp.max(scores, axis=-1, keepdims=True)
        exponent = jnp.exp(scores - row_top)
        row_total = jnp.sum(exponent, axis=-1, keepdims=True)
        softmax_out = (exponent / row_total).astype(jnp.bfloat16)
        context = jnp.einsum(
            "bhqk,bkhd->bqhd", softmax_out, qkv_block[:, :, 2], preferred_element_type=jnp.float32
        )
        return (context.astype(jnp.bfloat16), (row_top + jnp.log(row_total))[..., 0])

    def attend_back(packed):
        qkv_block, valid_keys, log_block, grad_block = packed
        scores = block_scores(qkv_block, valid_keys)
        softmax_out = jnp.exp(scores - log_block[..., None])
        grad_values = jnp.einsum(
            "bhqk,bqhd->bkhd",
            softmax_out.astype(jnp.bfloat16),
            grad_block,
            preferred_element_type=jnp.float32,
        )
        grad_soft = jnp.einsum(
            "bqhd,bkhd->bhqk", grad_block, qkv_block[:, :, 2], preferred_element_type=jnp.float32
        )
        grad_scores = softmax_out * (
            grad_soft - jnp.sum(grad_soft * softmax_out, axis=-1, keepdims=True)
        )
        scores_low = grad_scores.astype(jnp.bfloat16)
        grad_query = (
            jnp.einsum(
                "bhqk,bkhd->bqhd",
                scores_low,
                qkv_block[:, :, 1],
                preferred_element_type=jnp.float32,
            )
            * score_scale
        )
        grad_keys = (
            jnp.einsum(
                "bhqk,bqhd->bkhd",
                scores_low,
                qkv_block[:, :, 0],
                preferred_element_type=jnp.float32,
            )
            * score_scale
        )
        return jnp.stack([grad_query, grad_keys, grad_values], axis=2).astype(jnp.bfloat16)

    gathered = lax.all_gather(weights.astype(jnp.bfloat16), ("dp", "shard"), axis=0, tiled=True)
    first_mats = (
        gathered[:, : 3 * model_width],
        gathered[:, 3 * model_width : 4 * model_width],
        gathered[:, 4 * model_width : 8 * model_width],
        gathered[:, 8 * model_width :].reshape(4 * model_width, model_width),
    )
    w_qkv, w_out, w_in, w_down = first_mats
    qkv_low = (jnp.dot(token_low, w_qkv, preferred_element_type=jnp.float32) + qkv_bias).astype(
        jnp.bfloat16
    )
    qkv_blocks = qkv_low.reshape(block_count, block_slots, SLOT, 3, HEADS, head_size)
    contexts, log_total = lax.map(attend_block, (qkv_blocks, key_blocks))
    context_low = contexts.reshape(row_count, model_width)
    attention = jnp.dot(context_low, w_out, preferred_element_type=jnp.float32) + vectors[2]
    hidden_one, normed_one, inverse_one = norm_forward(tokens + attention, vectors[3], vectors[4])
    hidden_low = hidden_one.astype(jnp.bfloat16)
    pre_act = jnp.dot(hidden_low, w_in, preferred_element_type=jnp.float32) + ffn_bias
    act_low = jax.nn.gelu(pre_act, approximate=False).astype(jnp.bfloat16)
    ffn_out = jnp.dot(act_low, w_down, preferred_element_type=jnp.float32) + vectors[5]
    result, normed_two, inverse_two = norm_forward(hidden_one + ffn_out, vectors[6], vectors[7])
    first_kept = (
        qkv_blocks,
        log_total,
        context_low,
        normed_one,
        inverse_one,
        hidden_low,
        pre_act,
        act_low,
        normed_two,
        inverse_two,
        result,
    )
    output = first_kept[10]
    w_qkv, w_out, w_in, w_down = first_mats
    (
        qkv_blocks,
        log_total,
        context_low,
        normed_one,
        inverse_one,
        hidden_low,
        pre_act,
        act_low,
        normed_two,
        inverse_two,
    ) = first_kept[:10]
    grad_result = cotangent * row_weight
    grad_two, grad_gain_two, grad_shift_two = norm_backward(
        grad_result, normed_two, inverse_two, vectors[6]
    )
    grad_ffn_low = grad_two.astype(jnp.bfloat16)
    grad_bias_down = jnp.sum(grad_ffn_low, axis=0, dtype=jnp.float32)
    grad_down = jnp.einsum("tf,td->fd", act_low, grad_ffn_low, preferred_element_type=jnp.float32)
    grad_act = jnp.einsum("td,fd->tf", grad_ffn_low, w_down, preferred_element_type=jnp.float32)
    grad_pre_low = (grad_act * gelu_slope(pre_act)).astype(jnp.bfloat16)
    grad_bias_in = jnp.sum(grad_pre_low, axis=0, dtype=jnp.float32)
    grad_in = jnp.einsum("td,tf->df", hidden_low, grad_pre_low, preferred_element_type=jnp.float32)
    grad_hidden = grad_two + jnp.einsum(
        "tf,df->td", grad_pre_low, w_in, preferred_element_type=jnp.float32
    )
    grad_residual, grad_gain_one, grad_shift_one = norm_backward(
        grad_hidden, normed_one, inverse_one, vectors[3]
    )
    grad_attn_low = grad_residual.astype(jnp.bfloat16)
    grad_bias_out = jnp.sum(grad_attn_low, axis=0, dtype=jnp.float32)
    grad_out = jnp.einsum(
        "tc,td->cd", context_low, grad_attn_low, preferred_element_type=jnp.float32
    )
    grad_context = jnp.einsum(
        "td,cd->tc", grad_attn_low, w_out, preferred_element_type=jnp.float32
    ).astype(jnp.bfloat16)
    grad_blocks = grad_context.reshape(block_count, block_slots, SLOT, HEADS, head_size)
    grad_qkv_low = lax.map(attend_back, (qkv_blocks, key_blocks, log_total, grad_blocks)).reshape(
        row_count, 3 * model_width
    )
    grad_bias_qkv = jnp.sum(grad_qkv_low, axis=0, dtype=jnp.float32)
    grad_qkv = jnp.einsum("td,te->de", token_low, grad_qkv_low, preferred_element_type=jnp.float32)
    input_grad = grad_residual + jnp.einsum(
        "te,de->td", grad_qkv_low, w_qkv, preferred_element_type=jnp.float32
    )
    vector_grad = jnp.concatenate(
        [
            jnp.stack(
                [
                    grad_bias_qkv[:model_width],
                    grad_bias_qkv[2 * model_width :],
                    grad_bias_out,
                    grad_gain_one,
                    grad_shift_one,
                    grad_bias_down,
                    grad_gain_two,
                    grad_shift_two,
                ]
            ),
            grad_bias_in.reshape(4, model_width),
        ],
        axis=0,
    )
    qkv_shard, out_shard, in_shard, down_shard = (
        lax.psum_scatter(grad_qkv, ("dp", "shard"), scatter_dimension=0, tiled=True),
        lax.psum_scatter(grad_out, ("dp", "shard"), scatter_dimension=0, tiled=True),
        lax.psum_scatter(grad_in, ("dp", "shard"), scatter_dimension=0, tiled=True),
        lax.psum_scatter(
            grad_down.reshape(model_width, 4 * model_width),
            ("dp", "shard"),
            scatter_dimension=0,
            tiled=True,
        ),
    )
    vector_total = lax.psum(vector_grad, ("dp", "shard"))
    grad_shard = jnp.concatenate([qkv_shard, out_shard, in_shard, down_shard], axis=1)
    correction = 1.0 - 0.5**STEP
    new_first = 0.5 * moment1 + 0.5 * grad_shard
    new_second = 0.5 * moment2 + 0.5 * grad_shard * grad_shard
    update = new_first / correction / (jnp.sqrt(new_second / correction) + 1e-06) + 0.01 * weights
    column_edges = (0, 3 * model_width, 4 * model_width, 8 * model_width, 12 * model_width)
    pair_rows = []
    for group_index in range(4):
        weight_part = weights[:, column_edges[group_index] : column_edges[group_index + 1]]
        update_part = update[:, column_edges[group_index] : column_edges[group_index + 1]]
        pair_rows.append(
            jnp.stack([jnp.sum(weight_part * weight_part), jnp.sum(update_part * update_part)])
        )
    pair_squares = jnp.stack(pair_rows)
    pair_total = lax.psum(pair_squares, ("dp", "shard"))
    norm_pairs = jnp.sqrt(pair_total)
    trust_ratio = norm_pairs[:, 0] / (norm_pairs[:, 1] + 1e-06)
    column_trust = jnp.concatenate(
        [
            jnp.ones((column_edges[group_index + 1] - column_edges[group_index],), jnp.float32)
            * trust_ratio[group_index]
            for group_index in range(4)
        ]
    )
    new_weights = weights - 0.3 * column_trust * update
    vec_first = 0.5 * vec_moment1 + 0.5 * vector_total
    vec_second = 0.5 * vec_moment2 + 0.5 * vector_total * vector_total
    new_vectors = vectors - 0.3 * (vec_first / correction) / (
        jnp.sqrt(vec_second / correction) + 1e-06
    )
    return (
        output,
        input_grad,
        new_first,
        new_second,
        new_weights,
        vec_first,
        vec_second,
        new_vectors,
        norm_pairs,
        trust_ratio,
    )


def solution(mesh):
    in_specs = (
        P(("dp", "shard"), None),
        P(("dp", "shard"), None),
        P(("dp", "shard")),
        P(("dp", "shard")),
        P(("dp", "shard"), None),
        P(("dp", "shard"), None),
        P(("dp", "shard"), None),
        P(),
        P(),
        P(),
    )
    out_specs = (
        P(("dp", "shard"), None),
        P(("dp", "shard"), None),
        P(("dp", "shard"), None),
        P(("dp", "shard"), None),
        P(("dp", "shard"), None),
        P(),
        P(),
        P(),
        P(),
        P(),
    )
    return jax.shard_map(local, mesh=mesh, in_specs=in_specs, out_specs=out_specs, check_vma=False)
```

profile of v0, /device:TPU:0, one launch (start us, length us, event | category | flops | bytes accessed | tf_op | source)
XLA Modules:
  0.0 986.2 jit_solution(16578343813618891168)
XLA Ops:
  12.9 5.2 copy.65
  23.4 94.0 %all-gather.2.cloned.1.call-done = bf16[768,9216]{1,0:T(8,128)(2,1)} async-done(((bf16[24,9216]{1,0:T(8,128)(2,1)}), bf16[768,9216]{1,0:T(8,128)(2,1)}) %all-gather.2.cloned.1.call-update) | async-done | bytes 14155792 | tf_op jit(solution)/shard_map/all_gather | solution.py:123
  117.4 4.8 slice.153
  122.3 8.5 reshape.224
  130.7 8.0 fusion.47
  138.8 16.7 %reshape.233 = bf16[2,2,288,3,12,64]{5,4,3,2,1,0:T(8,128)(2,1)} reshape(bf16[1152,2304]{1,0:T(8,128)(2,1)} %fusion.47) | data formatting | bytes 10616832 | tf_op jit(solution)/shard_map/reshape | solution.py:134
  155.5 18.8 %copy.61 = bf16[2,2,288,3,12,64]{2,5,4,1,3,0:T(8,128)(2,1)} copy(bf16[2,2,288,3,12,64]{5,4,3,2,1,0:T(8,128)(2,1)} %reshape.233) | data formatting | bytes 10616832 | tf_op jit(solution)/shard_map/while | solution.py:135
  174.3 28.2 %while.22 = (s32[]{:T(128)}, bf16[2,2,288,12,64]{2,1,0,4,3:T(2,128)(2,1)}, f32[2,2,12,288]{3,2,1,0:T(8,128)}, bf16[2,2,288,3,12,64]{2,5,4,1,3,0:T(8,128)(2,1)}, pred[2,2,288]{2,1,0:T(4,128)(4,1)S(1)}, /*index=5*/s32[]{:T(128)}) while((s32[]{:T(128)}, bf16[2,2,288,12,64]{2,1,0,4,3:T(2,128)(2,1)}, f32[2,2,12,288]{3,2,1,0:T(8,128)}, ...), condition=%wide.region_3.4_spmd, body=%wide.region_0.3_spmd.sunk | while | flops 533931264 | bytes 53565324 | solution.py:135
  202.5 6.3 reshape.223
  213.3 42.6 %fusion.35 = (bf16[1152,3072]{1,0:T(8,128)(2,1)}, f32[1152,3072]{1,0:T(8,128)}) fusion(f32[3072]{0:T(1024)S(1)} %copy-done.35, bf16[768,9216]{1,0:T(8,128)(2,1)} %all-gather.2.cloned.1.call-done, f32[1152,768]{0,1:T(8,128)S(1)} %get-tuple-element.204, f32[768]{0:T(1024)S(1)} %copy-done.36, f32[768]{0:T(1024)S(1)} %copy-done.29, ...), kind=kOutput, calls=%fused_computation.55 | convolution fusion | flops 5673811968 | bytes 29518848 | tf_op jit(solution)/shard_map/dot_general | solution.py:140
  256.0 10.3 %fusion.86 = (f32[1152]{0:T(1024)S(1)}, f32[1152,768]{0,1:T(8,128)S(1)}) fusion(f32[768]{0:T(1024)S(1)} %copy-done.37, bf16[1152,3072]{1,0:T(8,128)(2,1)} %get-tuple-element.205, bf16[3072,768]{1,0:T(8,128)(2,1)S(1)} %bitcast.145, f32[768]{0:T(1024)S(1)} %copy-done.36, f32[768]{0:T(1024)S(1)} %copy-done.29, f32[1152]{0:T(1024)S(1)} %add_rsqrt_fusion.1, ...), kind=kOutput, calls=%fused_computation.180 | convolution fusion | flops 5442010112 | bytes 18897408 | tf_op jit(solution)/shard_map/dot_general | solution.py:142
  274.1 15.4 %convert_reduce_fusion = (f32[3072]{0:T(1024)}, bf16[1152,3072]{1,0:T(8,128)(2,1)}) fusion(f32[1152,3072]{1,0:T(8,128)} %get-tuple-element.206, bf16[3072,768]{1,0:T(8,128)(2,1)S(1)} %bitcast.145, f32[1152,768]{0,1:T(8,128)S(1)} %get-tuple-element.186), kind=kOutput, calls=%fused_computation.60 | convolution fusion | flops 5479166976 | bytes 29503488 | tf_op jit(solution)/shard_map/td,fd->tf/dot_general | solution.py:178
  289.5 11.9 %multiply_reduce_fusion.2 = (f32[768]{0:T(1024)}, f32[1152]{0:T(1024)S(1)}, f32[1152]{0:T(1024)S(1)}, f32[768]{0:T(1024)}, f32[1152,768]{0,1:T(8,128)S(1)}) fusion(f32[1152,768]{0,1:T(8,128)S(1)} %get-tuple-element.204, f32[1152]{0:T(1024)S(1)} %add_rsqrt_fusion.1, f32[1152]{0:T(1024)S(1)} %broadcast_multiply_fusion.5, f32[768]{0:T(1024)S(1)} %copy-done.29, ...), kind=kOutput, calls=%fused_computation.93 | convolution fusion | flops 5444661248 | bytes 22440960 | tf_op jit(solution)/shard_map/tf,df->td/dot_general | solution.py:182
  312.6 6.1 copy.69
  318.8 45.9 %while.23 = (s32[]{:T(128)}, bf16[2,2,288,3,12,64]{2,5,4,1,3,0:T(8,128)(2,1)}, bf16[2,2,288,3,12,64]{2,5,4,1,3,0:T(8,128)(2,1)}, pred[2,2,288]{2,1,0:T(4,128)(4,...) while((s32[]{:T(128)}, ...), condition=%wide.region_14.15_spmd, body=%wide.region_12.14_spmd.sunk | while | flops 1314047232 | bytes 108031864 | solution.py:197
  327.7 5.0 multiply_reduce_fusion.15
  350.5 5.0 multiply_reduce_fusion.15
  364.7 14.1 %copy.70 = bf16[2,2,288,3,12,64]{2,1,0,5,4,3:T(2,128)(2,1)} copy(bf16[2,2,288,3,12,64]{2,5,4,1,3,0:T(8,128)(2,1)} %get-tuple-element.72) | data formatting | bytes 10616832 | tf_op jit(solution)/shard_map/while | solution.py:197
  378.9 14.9 %reshape.226 = bf16[1152,2304]{0,1:T(8,128)(2,1)} reshape(bf16[2,2,288,3,12,64]{2,1,0,5,4,3:T(2,128)(2,1)} %copy.70) | data formatting | bytes 10616832 | tf_op jit(solution)/shard_map/reshape | solution.py:197
  393.8 9.3 convolution_bitcast_fusion
  403.0 8.0 copy.85
  411.2 5.8 fusion.71
  417.1 12.2 %fusion.77 = f32[768,3072]{1,0:T(8,128)} fusion(bf16[1152,3072]{1,0:T(8,128)(2,1)} %get-tuple-element.211, f32[1152,768]{0,1:T(8,128)S(1)} %copy-done.6, f32[768]{0:T(1024)} %get-tuple-element.150, f32[768]{0:T(1024)} %get-tuple-element.151, f32[1152]{0:T(1024)S(1)} %copy-done.28, f32[1152]{0:T(1024)S(1)} %copy-done.25), kind=kOutput, calls=%fused_computation.175 | convolution fusion | flops 5440241664 | bytes 20069376 | tf_op jit(solution)/shard_map/td,tf->df/dot_general | solution.py:181
  431.4 10.8 %fusion.74 = f32[3072,768]{1,0:T(8,128)} fusion(bf16[1152,3072]{1,0:T(8,128)(2,1)} %get-tuple-element.205, f32[1152,768]{0,1:T(8,128)S(1)} %copy-done.14), kind=kOutput, calls=%fused_computation.172 | convolution fusion | flops 5436702720 | bytes 20054016 | tf_op jit(solution)/shard_map/tf,td->fd/dot_general | solution.py:177
  442.2 11.7 %reshape.227 = f32[768,3072]{1,0:T(8,128)} reshape(f32[3072,768]{1,0:T(8,128)} %fusion.74) | data formatting | bytes 18874368 | tf_op jit(solution)/shard_map/reshape | solution.py:228
  469.5 10.1 %convolution_add_fusion.4 = f32[1152,768]{0,1:T(8,128)} fusion(f32[1152,768]{0,1:T(8,128)S(1)} %copy-done.12, bf16[1152,2304]{0,1:T(8,128)(2,1)} %reshape.226, bf16[768,9216]{1,0:T(8,128)(2,1)} %all-gather.2.cloned.1.call-done), kind=kOutput, calls=%fused_computation.89 | convolution fusion | flops 4077748224 | bytes 15925248 | tf_op jit(solution)/shard_map/te,de->td/dot_general | solution.py:202
  479.6 5.2 copy.74
  488.3 40.2 %reduce-scatter.13.cloned.1.call-done = f32[24,2304]{1,0:T(8,128)} async-done(((f32[768,2304]{1,0:T(8,128)}), f32[24,2304]{1,0:T(8,128)}) %reduce-scatter.13.cloned.1.call-update) | async-done | bytes 221200 | tf_op jit(solution)/shard_map/reduce_scatter | solution.py:224
  530.1 102.8 %reduce-scatter.7.cloned.1.call-done = f32[24,768]{1,0:T(8,128)} async-done(((f32[768,768]{1,0:T(8,128)}), f32[24,768]{1,0:T(8,128)}) %reduce-scatter.7.cloned.1.call-update) | async-done | bytes 73744 | tf_op jit(solution)/shard_map/reduce_scatter | solution.py:225
  634.5 138.9 %reduce-scatter.9.cloned.1.call-done = f32[24,3072]{1,0:T(8,128)} async-done(((f32[768,3072]{1,0:T(8,128)}), f32[24,3072]{1,0:T(8,128)}) %reduce-scatter.9.cloned.1.call-update) | async-done | bytes 294928 | tf_op jit(solution)/shard_map/reduce_scatter | solution.py:226
  775.1 139.7 %reduce-scatter.11.cloned.1.call-done = f32[24,3072]{1,0:T(8,128)} async-done(((f32[768,3072]{1,0:T(8,128)}), f32[24,3072]{1,0:T(8,128)}) %reduce-scatter.11.cloned.1.call-update) | async-done | bytes 294928 | tf_op jit(solution)/shard_map/reduce_scatter | solution.py:227
  930.6 40.3 %all-reduce = (f32[4,2]{1,0:T(4,128)S(1)}, f32[12,768]{1,0:T(8,128)S(1)}) all-reduce(f32[4,2]{1,0:T(4,128)S(1)} %pad_maximum_fusion.1, f32[12,768]{1,0:T(8,128)} %concatenate.27), channel_id=1, replica_groups=mesh['dp'=8,'shard'=4] {'dp','shard'}, use_global_device_ids=true, to_apply=%region_27.28 | all-reduce | flops 9224 | bytes 73792 | tf_op jit(solution)/shard_map/psum | solution.py:249
  (209 shorter events, 148.2 us)
Async XLA Ops:
  7.2 10.9 %copy-start.9 = (f32[1152,768]{1,0:T(8,128)S(1)}, f32[1152,768]{1,0:T(8,128)}, u32[]{:S(2)}) copy-start(f32[1152,768]{1,0:T(8,128)} %param.14) | copy-start | bytes 10616836
  7.2 110.3 %all-gather.2.cloned.1.call-start = ((), (), s32[]{:S(2)}) async-start(), calls=%async_computation.4 | async-start | bytes 14598144 | tf_op jit(solution)/shard_map/all_gather | solution.py:123
  9.4 519.1 %reduce-scatter.13.cloned.1.call-start = ((), (), s32[]{:S(2)}) async-start(), calls=%async_computation.8 | async-start | bytes 7299072 | tf_op jit(solution)/shard_map/reduce_scatter | solution.py:224
  174.3 34.6 %copy-start.15 = (f32[1152,768]{0,1:T(8,128)S(1)}, f32[1152,768]{0,1:T(8,128)}, u32[]{:S(2)}) copy-start(f32[1152,768]{0,1:T(8,128)} %copy.63) | copy-start | bytes 10616836
  174.3 34.6 %copy-start.38 = (f32[768]{0:T(1024)S(1)}, f32[768]{0:T(1024)}, u32[]{:S(2)}) copy-start(f32[768]{0:T(1024)} %get-tuple-element.152) | copy-start | bytes 9220
  202.5 10.3 %copy-start.21 = (pred[2,2,288]{2,1,0:T(4,128)(4,1)}, pred[2,2,288]{2,1,0:T(4,128)(4,1)S(1)}, u32[]{:S(2)}) copy-start(pred[2,2,288]{2,1,0:T(4,128)(4,1)S(1)} %get-tuple-element.349) | copy-start | bytes 3460
  208.9 4.4 copy-start.35
  208.9 4.4 copy-start.36
  208.9 47.0 %slice-start = ((s8[4718592]{0:T(1024)(128)(4,1)}), s8[4194304]{0:T(1024)(128)(4,1)S(1)}, s32[]{:S(2)}) async-start(s8[4718592]{0:T(1024)(128)(4,1)} %bitcast.144), calls=%async_computation.9 | async-start | bytes 8388608
  212.8 88.7 %copy-start.5 = (f32[1152,768]{0,1:T(8,128)}, f32[1152,768]{0,1:T(8,128)S(1)}, u32[]{:S(2)}) copy-start(f32[1152,768]{0,1:T(8,128)S(1)} %get-tuple-element.204) | copy-start | bytes 10616836
  212.8 88.7 %copy-start.24 = (f32[1152]{0:T(1024)}, f32[1152]{0:T(1024)S(1)}, u32[]{:S(2)}) copy-start(f32[1152]{0:T(1024)S(1)} %broadcast_multiply_fusion.5) | copy-start | bytes 13828
  213.2 88.2 %copy-start.27 = (f32[1152]{0:T(1024)}, f32[1152]{0:T(1024)S(1)}, u32[]{:S(2)}) copy-start(f32[1152]{0:T(1024)S(1)} %add_rsqrt_fusion.1) | copy-start | bytes 13828
  213.3 42.7 %slice-start.1 = ((s8[4718592]{0:T(1024)(128)(4,1)}), s8[524288]{0:T(1024)(128)(4,1)S(1)}, s32[]{:S(2)}) async-start(s8[4718592]{0:T(1024)(128)(4,1)} %bitcast.144), calls=%async_computation.10 | async-start | bytes 1048576
  213.3 42.7 %copy-start.37 = (f32[768]{0:T(1024)S(1)}, f32[768]{0:T(1024)}, u32[]{:S(2)}) copy-start(f32[768]{0:T(1024)} %get-tuple-element.149) | copy-start | bytes 9220
  256.0 10.8 %copy-start.23 = (f32[1152]{0:T(1024)S(1)}, f32[1152]{0:T(1024)}, u32[]{:S(2)}) copy-start(f32[1152]{0:T(1024)} %reshape.229) | copy-start | bytes 13828
  256.0 10.8 %copy-start.26 = (f32[768]{0:T(1024)S(1)}, f32[768]{0:T(1024)}, u32[]{:S(2)}) copy-start(f32[768]{0:T(1024)} %get-tuple-element.148) | copy-start | bytes 9220
  274.1 15.4 %copy-start.13 = (f32[1152,768]{0,1:T(8,128)}, f32[1152,768]{0,1:T(8,128)S(1)}, u32[]{:S(2)}) copy-start(f32[1152,768]{0,1:T(8,128)S(1)} %get-tuple-element.186) | copy-start | bytes 10616836
  312.6 6.2 copy-start.20
  312.6 6.2 copy-start.22
  319.2 4.8 copy-start.2
  342.0 4.8 copy-start.2
  378.9 14.9 %copy-start.10 = (f32[1152,768]{1,0:T(8,128)S(1)}, f32[1152,768]{1,0:T(8,128)}, u32[]{:S(2)}) copy-start(f32[1152,768]{1,0:T(8,128)} %param.14) | copy-start | bytes 10616836
  411.1 6.0 copy-start.6
  411.1 6.0 copy-start.25
  411.1 6.0 copy-start.28
  411.1 221.8 %reduce-scatter.7.cloned.1.call-start = ((), (), s32[]{:S(2)}) async-start(), calls=%async_computation.5 | async-start | bytes 2433024 | tf_op jit(solution)/shard_map/reduce_scatter | solution.py:225
  417.0 356.4 %reduce-scatter.9.cloned.1.call-start = ((), (), s32[]{:S(2)}) async-start(), calls=%async_computation.6 | async-start | bytes 9732096 | tf_op jit(solution)/shard_map/reduce_scatter | solution.py:226
  429.3 485.5 %reduce-scatter.11.cloned.1.call-start = ((), (), s32[]{:S(2)}) async-start(), calls=%async_computation.7 | async-start | bytes 9732096 | tf_op jit(solution)/shard_map/reduce_scatter | solution.py:227
  453.9 5.1 copy-start.33
  457.1 12.4 %copy-start.12 = (f32[1152,768]{0,1:T(8,128)S(1)}, f32[1152,768]{0,1:T(8,128)}, u32[]{:S(2)}) copy-start(f32[1152,768]{0,1:T(8,128)} %copy-done.11) | copy-start | bytes 10616836
  479.6 6.7 copy-start.34
  484.8 442.9 %copy-start.4 = (f32[1152,768]{0,1:T(8,128)S(1)}, f32[1152,768]{0,1:T(8,128)}, u32[]{:S(2)}) copy-start(f32[1152,768]{0,1:T(8,128)} %get-tuple-element.196) | copy-start | bytes 10616836
  (21 other events, 52.4 us)
Sparse Core Ops, SparseCore 0:
  11.5 105.9 all-gather.1
  411.2 117.2 reduce-scatter.12
  534.6 98.2 reduce-scatter.6
  638.7 134.6 reduce-scatter.8
  780.1 134.6 reduce-scatter.10
where the time goes:
time: 1010 us; the launch traced here: 986 us
  waiting for transfers between devices  516 us (51%)
  local copies, waits for them, and re-layouts  183 us (18%)
  matrix products  182 us (18%)
  other arithmetic  50 us (5%)
  blocking collectives  40.3 us (4%)
  between operations  14.4 us (1%)
    reduce_scatter x1, waiting for transfers between devices, local(): lax.psum_scatter(grad_down.reshape(model_width, 4 * model_width), ('dp',...  140 us
    reduce_scatter x1, waiting for transfers between devices, local(): lax.psum_scatter(grad_in, ('dp', 'shard'), scatter_dimension=0, tiled=True)  139 us
    reduce_scatter x1, waiting for transfers between devices, local(): lax.psum_scatter(grad_out, ('dp', 'shard'), scatter_dimension=0, tiled=True)  103 us
    all_gather x1, waiting for transfers between devices, local(): lax.all_gather(weights.astype(jnp.bfloat16), ('dp', 'shard'), axis=0, til...  94 us
    dot_general x1, matrix products, local(): jnp.dot(hidden_low, w_in, preferred_element_type=jnp.float32) + ffn_bias  42.6 us
    psum x1, blocking collectives, local(): pair_total = lax.psum(pair_squares, ('dp', 'shard'))  40.3 us
    reduce_scatter x1, waiting for transfers between devices, local(): lax.psum_scatter(grad_qkv, ('dp', 'shard'), scatter_dimension=0, tiled=True)  40.2 us
    unnamed x77, local copies, waits for them, and re-layouts  36.4 us
  transfers between devices with their start and end apart: 5, of which 5 were waited for; matrix products, arithmetic and copies ran while one was open for 9% of the time, Pallas kernels for 0%

commit v1 on v0

--- a/solution.py
+++ b/solution.py
@@ -1,6 +1,8 @@
 import jax
 import jax.numpy as jnp
 from jax import lax
+from jax.experimental import pallas as pl
+from jax.experimental.pallas import tpu as pltpu
 from jax.sharding import PartitionSpec as P
 
 HEADS = 12
@@ -32,7 +34,7 @@
     )
 
 
-def local(
+def plain(
     tokens,
     cotangent,
     lengths,
@@ -276,29 +278,443 @@
     )
 
 
+SUM = jnp.float32
+LOW = jnp.bfloat16
+PIECES = 12
+TILE = 768
+HALF = 384
+NEG = -1e9
+
+
+def dot(left, right, left_dim, right_dim):
+    return lax.dot_general(
+        left, right, (((left_dim,), (right_dim,)), ((), ())), preferred_element_type=SUM
+    )
+
+
+def slot_rows(slot):
+    return pl.ds(pl.multiple_of(slot * SLOT, SLOT), SLOT)
+
+
+def each(count, body):
+    def step(index, carry):
+        body(index)
+        return carry
+
+    lax.fori_loop(0, count, step, 0)
+
+
+def mean_lanes(values):
+    return jnp.mean(values, axis=-1, keepdims=True)
+
+
+def sum_rows(values):
+    return jnp.sum(values, axis=0, keepdims=True)
+
+
+def head_operands(query, key, valid):
+    lane = lax.broadcasted_iota(jnp.int32, query.shape, 1)
+    row = lax.broadcasted_iota(jnp.int32, query.shape, 0)
+    low_head = lane < 64
+    bias = jnp.where(row < valid, 0.0, NEG).astype(LOW)
+    scaled = query * jnp.asarray(0.125, LOW)
+    one, zero = jnp.ones_like(query), jnp.zeros_like(query)
+    queries = (
+        jnp.where(low_head, scaled, jnp.where(lane == 64, one, zero)),
+        jnp.where(low_head, jnp.where(lane == 0, one, zero), scaled),
+    )
+    keys = (
+        jnp.where(low_head, key, jnp.where(lane == 64, bias, zero)),
+        jnp.where(low_head, jnp.where(lane == 0, bias, zero), key),
+    )
+    return queries, keys, low_head
+
+
+def attend(unit, slot, valid, qkv, context, log_total):
+    rows = slot_rows(slot)
+    items = []
+    for half in range(2):
+        query, key, value = (
+            qkv[unit, rows, (3 * half + part) * 128 : (3 * half + part + 1) * 128]
+            for part in range(3)
+        )
+        queries, keys, low_head = head_operands(query, key, valid)
+        items += [(queries[head], keys[head], value) for head in range(2)]
+    scores = [dot(key, query, 1, 1) for query, key, _ in items]
+    results = []
+    for index, values in enumerate(scores):
+        top = jnp.max(values, axis=0, keepdims=True)
+        exponent = jnp.exp(values - top)
+        total = sum_rows(exponent)
+        log_total[unit, slot, index : index + 1, :] = top + jnp.log(total)
+        results.append((exponent * (1.0 / total)).astype(LOW))
+    results = [dot(probs, item[2], 0, 0) for probs, item in zip(results, items)]
+    for half in range(2):
+        lanes = pl.ds(pl.multiple_of((unit + 3 * half) * 128, 128), 128)
+        joined = jnp.where(low_head, results[2 * half], results[2 * half + 1])
+        context[rows, lanes] = joined.astype(LOW)
+
+
+def attend_back(unit, slot, valid, qkv, grad_context, log_total, vec_grad):
+    rows = slot_rows(slot)
+    items = []
+    for half in range(2):
+        query, key, value = (
+            qkv[unit, rows, (3 * half + part) * 128 : (3 * half + part + 1) * 128]
+            for part in range(3)
+        )
+        lanes = pl.ds(pl.multiple_of((unit + 3 * half) * 128, 128), 128)
+        grad = grad_context[rows, lanes]
+        queries, keys, low_head = head_operands(query, key, valid)
+        zero = jnp.zeros_like(grad)
+        grads = (jnp.where(low_head, grad, zero), jnp.where(low_head, zero, grad))
+        items += [
+            (queries[head], keys[head], grads[head], query, key, value, grad) for head in range(2)
+        ]
+    scores = [dot(item[1], item[0], 1, 1) for item in items]
+    grad_probs = [dot(item[5], item[2], 1, 1) for item in items]
+    probs, grad_value = [], []
+    for index, item in enumerate(items):
+        probs.append(jnp.exp(scores[index] - log_total[unit, slot, index : index + 1, :]))
+        grad_value.append(dot(probs[index].astype(LOW), item[6], 1, 0))
+    grad_key, grad_query = [], []
+    for index, item in enumerate(items):
+        inner = sum_rows(grad_probs[index] * probs[index])
+        low = (probs[index] * (grad_probs[index] - inner)).astype(LOW)
+        grad_key.append(dot(low, item[3], 1, 0))
+        grad_query.append(dot(low, item[4], 0, 0))
+    for half in range(2):
+        first, second = 2 * half, 2 * half + 1
+        lanes = pl.ds(pl.multiple_of((unit + 3 * half) * 128, 128), 128)
+        for part, parts, scale in (
+            (0, grad_query, 0.125),
+            (1, grad_key, 0.125),
+            (2, grad_value, 1.0),
+        ):
+            joined = (jnp.where(low_head, parts[first], parts[second]) * scale).astype(LOW)
+            qkv[unit, rows, (3 * half + part) * 128 : (3 * half + part + 1) * 128] = joined
+            if part != 1:
+                row = part // 2
+                vec_grad[row : row + 1, lanes] += sum_rows(joined.astype(SUM))
+
+
+def layer(
+    valid, tokens, cotangent, walls, vectors, qkv_bias, ffn_bias,
+    output, input_grad, pieces, vec_grad,
+    normed, token_low, qkv, context, hidden_low, act, slope, grad, grad_low, side, inverse,
+    log_total, mat, mat_low, in_sem, out_sem, mat_sem,
+):
+    def weight(piece):
+        return walls[piece]
+
+    cot_copy = pltpu.make_async_copy(cotangent, side, in_sem.at[0])
+    cot_copy.start()
+    tok_copy = pltpu.make_async_copy(tokens, normed, in_sem.at[1])
+    tok_copy.start()
+    tok_copy.wait()
+    vec_grad[...] = jnp.zeros_like(vec_grad)
+
+    def cast_slot(slot):
+        rows = slot_rows(slot)
+        token_low[rows, :] = normed[rows, :].astype(LOW)
+
+    each(4, cast_slot)
+
+    def project(unit):
+        def project_slot(slot):
+            rows = slot_rows(slot)
+            values = dot(token_low[rows, :], weight(unit), 1, 0) + qkv_bias[unit]
+            qkv[unit, rows, :] = values.astype(LOW)
+
+        each(4, project_slot)
+        each(4, lambda slot: attend(unit, slot, valid[slot], qkv, context, log_total))
+
+    each(3, project)
+
+    def attend_out(slot):
+        rows = slot_rows(slot)
+        values = normed[rows, :] + (dot(context[rows, :], weight(3), 1, 0) + vectors[2:3, :])
+        centred = values - mean_lanes(values)
+        inv = lax.rsqrt(mean_lanes(centred * centred) + 1e-05)
+        unit_values = centred * inv
+        normed[rows, :] = unit_values
+        inverse[rows, :] = jnp.broadcast_to(inv, (SLOT, 128))
+        hidden_low[rows, :] = (unit_values * vectors[3:4, :] + vectors[4:5, :]).astype(LOW)
+
+    each(4, attend_out)
+
+    def widen(chunk):
+        def widen_slot(slot):
+            rows = slot_rows(slot)
+            pre = dot(hidden_low[rows, :], weight(4 + chunk), 1, 0) + ffn_bias[chunk]
+            phi = 0.5 + 0.5 * lax.erf(pre * 0.7071067811865476)
+            act[chunk, rows, :] = (pre * phi).astype(LOW)
+            bell = jnp.exp(pre * pre * -0.5) * 0.3989422804014327
+            slope[chunk, rows, :] = (phi + pre * bell).astype(LOW)
+
+        each(4, widen_slot)
+
+    each(4, widen)
+    cot_copy.wait()
+
+    def narrow(slot):
+        rows = slot_rows(slot)
+        ffn = dot(act[0, rows, :], weight(8), 1, 0)
+        for chunk in range(1, 4):
+            ffn += dot(act[chunk, rows, :], weight(8 + chunk), 1, 0)
+        hidden = normed[rows, :] * vectors[3:4, :] + vectors[4:5, :]
+        values = hidden + (ffn + vectors[5:6, :])
+        centred = values - mean_lanes(values)
+        inv = lax.rsqrt(mean_lanes(centred * centred) + 1e-05)
+        unit_values = centred * inv
+        kept = lax.broadcasted_iota(jnp.int32, (SLOT, 1), 0) < valid[slot]
+        grad_out = jnp.where(kept, side[rows, :], 0.0)
+        side[rows, :] = unit_values * vectors[6:7, :] + vectors[7:8, :]
+        pltpu.make_async_copy(side.at[rows, :], output.at[rows, :], out_sem.at[slot]).start()
+        vec_grad[6:7, :] += sum_rows(grad_out * unit_values)
+        vec_grad[7:8, :] += sum_rows(grad_out)
+        scaled = grad_out * vectors[6:7, :]
+        result = inv * (
+            scaled - mean_lanes(scaled) - unit_values * mean_lanes(scaled * unit_values)
+        )
+        grad[rows, :] = result
+        low = result.astype(LOW)
+        grad_low[rows, :] = low
+        vec_grad[5:6, :] += sum_rows(low.astype(SUM))
+
+    each(4, narrow)
+
+    def piece_copy(index, piece):
+        slot = lax.rem(index, 2)
+        return pltpu.make_async_copy(mat_low.at[slot], pieces.at[piece], mat_sem.at[slot])
+
+    def emit(index, piece, left, right):
+        values = dot(left, right, 0, 0)
+
+        @pl.when(index >= 2)
+        def _():
+            piece_copy(index, piece).wait()
+
+        mat_low[lax.rem(index, 2)] = values.astype(LOW)
+        piece_copy(index, piece).start()
+
+    def back_chunk(chunk):
+        emit(2 * chunk, 8 + chunk, act[chunk], grad_low[...])
+
+        def back_slot(slot):
+            rows = slot_rows(slot)
+            values = dot(grad_low[rows, :], weight(8 + chunk), 1, 1)
+            low = (values * slope[chunk, rows, :].astype(SUM)).astype(LOW)
+            slope[chunk, rows, :] = low
+            row = pl.ds(8 + chunk, 1)
+            vec_grad[row, :] += sum_rows(low.astype(SUM))
+
+        each(4, back_slot)
+        emit(2 * chunk + 1, 4 + chunk, hidden_low[...], slope[chunk])
+
+    each(4, back_chunk)
+
+    def back_norm(slot):
+        rows = slot_rows(slot)
+        total = grad[rows, :]
+        for chunk in range(4):
+            total += dot(slope[chunk, rows, :], weight(4 + chunk), 1, 1)
+        unit_values = normed[rows, :]
+        vec_grad[3:4, :] += sum_rows(total * unit_values)
+        vec_grad[4:5, :] += sum_rows(total)
+        scaled = total * vectors[3:4, :]
+        inv = inverse[rows, 0:1]
+        result = inv * (
+            scaled - mean_lanes(scaled) - unit_values * mean_lanes(scaled * unit_values)
+        )
+        grad[rows, :] = result
+        low = result.astype(LOW)
+        grad_low[rows, :] = low
+        vec_grad[2:3, :] += sum_rows(low.astype(SUM))
+
+    each(4, back_norm)
+    emit(8, 3, context[...], grad_low[...])
+
+    def back_context(slot):
+        rows = slot_rows(slot)
+        context[rows, :] = dot(grad_low[rows, :], weight(3), 1, 1).astype(LOW)
+
+    each(4, back_context)
+
+    def back_unit(unit):
+        each(
+            4,
+            lambda slot: attend_back(unit, slot, valid[slot], qkv, context, log_total, vec_grad),
+        )
+        emit(9 + unit, unit, token_low[...], qkv[unit])
+
+    each(3, back_unit)
+
+    def back_tokens(slot):
+        rows = slot_rows(slot)
+        pltpu.make_async_copy(side.at[rows, :], output.at[rows, :], out_sem.at[slot]).wait()
+        total = grad[rows, :]
+        for unit in range(3):
+            total += dot(qkv[unit, rows, :], weight(unit), 1, 1)
+        side[rows, :] = total
+        pltpu.make_async_copy(side.at[rows, :], input_grad.at[rows, :], out_sem.at[slot]).start()
+
+    each(4, back_tokens)
+    for slot in range(4):
+        rows = slot_rows(slot)
+        pltpu.make_async_copy(side.at[rows, :], input_grad.at[rows, :], out_sem.at[slot]).wait()
+    piece_copy(10, 0).wait()
+    piece_copy(11, 0).wait()
+
+
+def permute_columns(shard):
+    rows = shard.shape[0]
+    first = shard[:, :2304].reshape(rows, 3, 2, 3, 128).transpose(3, 0, 2, 1, 4)
+    second = shard[:, 2304:3072].reshape(1, rows, TILE)
+    third = shard[:, 3072:6144].reshape(rows, TILE, 4).transpose(2, 0, 1)
+    fourth = shard[:, 6144:].reshape(rows, 4, TILE).transpose(1, 0, 2)
+    return jnp.concatenate([first.reshape(3, rows, TILE), second, third, fourth], axis=0)
+
+
+def restore_columns(pieces):
+    rows = pieces.shape[1]
+    first = pieces[:3].reshape(3, rows, 2, 3, 128).transpose(1, 3, 2, 0, 4)
+    third = pieces[4:8].transpose(1, 2, 0)
+    fourth = pieces[8:].transpose(1, 0, 2)
+    return jnp.concatenate(
+        [
+            first.reshape(rows, 2304),
+            pieces[3],
+            third.reshape(rows, 3072),
+            fourth.reshape(rows, 3072),
+        ],
+        axis=1,
+    )
+
+
+def run_layer(tokens, cotangent, valid, walls, vectors):
+    rows = tokens.shape[0]
+    zero = jnp.zeros((TILE,), SUM)
+    qkv_bias = jnp.stack([vectors[0], zero, vectors[1]]).reshape(3, 2, 3, 128)
+    qkv_bias = qkv_bias.transpose(2, 1, 0, 3).reshape(3, 1, TILE)
+    ffn_bias = vectors[8:12].reshape(TILE, 4).T.reshape(4, 1, TILE)
+    vmem = pl.BlockSpec(memory_space=pltpu.VMEM)
+    smem = pl.BlockSpec(memory_space=pltpu.SMEM)
+    hbm = pl.BlockSpec(memory_space=pl.ANY)
+    full = lambda *shape: pltpu.VMEM(shape, SUM)
+    low = lambda *shape: pltpu.VMEM(shape, LOW)
+    return pl.pallas_call(
+        layer,
+        out_shape=[
+            jax.ShapeDtypeStruct((rows, TILE), SUM),
+            jax.ShapeDtypeStruct((rows, TILE), SUM),
+            jax.ShapeDtypeStruct((PIECES, TILE, TILE), LOW),
+            jax.ShapeDtypeStruct((16, TILE), SUM),
+        ],
+        in_specs=[smem, hbm, hbm, vmem, vmem, vmem, vmem],
+        out_specs=[hbm, hbm, hbm, vmem],
+        scratch_shapes=[
+            full(rows, TILE),
+            low(rows, TILE),
+            low(3, rows, TILE),
+            low(rows, TILE),
+            low(rows, TILE),
+            low(4, rows, TILE),
+            low(4, rows, TILE),
+            full(rows, TILE),
+            low(rows, TILE),
+            full(rows, TILE),
+            full(rows, 128),
+            full(3, 4, 4, SLOT),
+            full(8, 128),
+            low(2, TILE, TILE),
+            pltpu.SemaphoreType.DMA((2,)),
+            pltpu.SemaphoreType.DMA((4,)),
+            pltpu.SemaphoreType.DMA((2,)),
+        ],
+        compiler_params=pltpu.CompilerParams(vmem_limit_bytes=63 * 2**20),
+        cost_estimate=pl.CostEstimate(
+            flops=60 * 10**9, bytes_accessed=60 * 10**6, transcendentals=10**7
+        ),
+    )(valid, tokens, cotangent, walls, vectors, qkv_bias, ffn_bias)
+
+
+def fused(
+    tokens,
+    cotangent,
+    lengths,
+    null_flags,
+    weights,
+    moment1,
+    moment2,
+    vectors,
+    vec_moment1,
+    vec_moment2,
+):
+    axes = ("dp", "shard")
+    valid = jnp.where(null_flags == 1, QLEN, lengths).astype(jnp.int32)
+    low = permute_columns(weights.astype(LOW))
+    walls = lax.all_gather(low, axes, axis=1, tiled=True)
+    output, input_grad, pieces, vec_grad = run_layer(tokens, cotangent, valid, walls, vectors)
+    shard = lax.psum_scatter(pieces, axes, scatter_dimension=1, tiled=True)
+    grad_shard = restore_columns(shard.astype(SUM))
+    vec_total = lax.psum(vec_grad, axes)
+    ffn_rows = vec_total[8:12].T.reshape(4, TILE)
+    vec_total = jnp.concatenate([vec_total[:8], ffn_rows], axis=0)
+    return (output, input_grad) + optimize(
+        grad_shard, vec_total, weights, moment1, moment2, vectors, vec_moment1, vec_moment2
+    )
+
+
+def optimize(
+    grad_shard, vec_total, weights, moment1, moment2, vectors, vec_moment1, vec_moment2
+):
+    correction = 1.0 - 0.5**STEP
+    new_first = 0.5 * moment1 + 0.5 * grad_shard
+    new_second = 0.5 * moment2 + 0.5 * grad_shard * grad_shard
+    update = new_first / correction / (jnp.sqrt(new_second / correction) + 1e-06) + 0.01 * weights
+    edges = (0, 2304, 3072, 6144, 9216)
+    squares = jnp.stack(
+        [
+            jnp.stack(
+                [
+                    jnp.sum(jnp.square(values[:, edges[index] : edges[index + 1]]))
+                    for values in (weights, update)
+                ]
+            )
+            for index in range(4)
+        ]
+    )
+    norm_pairs = jnp.sqrt(lax.psum(squares, ("dp", "shard")))
+    trust = norm_pairs[:, 0] / (norm_pairs[:, 1] + 1e-06)
+    column = jnp.arange(weights.shape[1])
+    column_trust = jnp.where(
+        column < edges[1],
+        trust[0],
+        jnp.where(column < edges[2], trust[1], jnp.where(column < edges[3], trust[2], trust[3])),
+    )
+    new_weights = weights - 0.3 * column_trust * update
+    vec_first = 0.5 * vec_moment1 + 0.5 * vec_total
+    vec_second = 0.5 * vec_moment2 + 0.5 * vec_total * vec_total
+    new_vectors = vectors - 0.3 * (vec_first / correction) / (
+        jnp.sqrt(vec_second / correction) + 1e-06
+    )
+    return (
+        new_first,
+        new_second,
+        new_weights,
+        vec_first,
+        vec_second,
+        new_vectors,
+        norm_pairs,
+        trust,
+    )
+
+
 def solution(mesh):
-    in_specs = (
-        P(("dp", "shard"), None),
-        P(("dp", "shard"), None),
-        P(("dp", "shard")),
-        P(("dp", "shard")),
-        P(("dp", "shard"), None),
-        P(("dp", "shard"), None),
-        P(("dp", "shard"), None),
-        P(),
-        P(),
-        P(),
-    )
-    out_specs = (
-        P(("dp", "shard"), None),
-        P(("dp", "shard"), None),
-        P(("dp", "shard"), None),
-        P(("dp", "shard"), None),
-        P(("dp", "shard"), None),
-        P(),
-        P(),
-        P(),
-        P(),
-        P(),
-    )
-    return jax.shard_map(local, mesh=mesh, in_specs=in_specs, out_specs=out_specs, check_vma=False)
+    split = P(("dp", "shard"), None)
+    flat = P(("dp", "shard"))
+    in_specs = (split, split, flat, flat, split, split, split, P(), P(), P())
+    out_specs = (split,) * 5 + (P(),) * 5
+    body = fused if mesh.shape["dp"] == 8 and mesh.shape["shard"] == 4 else plain
+    return jax.shard_map(body, mesh=mesh, in_specs=in_specs, out_specs=out_specs, check_vma=False)

time: 1010 us -> 475 us (0.47); the launches traced: 986 us -> 475 us
  waiting for transfers between devices: 516 us -> 262 us
  matrix products: 182 us -> 0 us
  local copies, waits for them, and re-layouts: 183 us -> 21.7 us
  Pallas kernels: 0 us -> 116 us
  other arithmetic: 50 us -> 20.3 us
    reduce_scatter x4 -> x0, waiting for transfers between devices: 422 us -> none  [the longest x1 140 us: local(): lax.psum_scatter(grad_down.reshape(model_width, 4 * model_width), ('dp',...]
    dot_general x26 -> x0, matrix products: 182 us -> none  [the longest x1 42.6 us: local(): jnp.dot(hidden_low, w_in, preferred_element_type=jnp.float32) + ffn_bias]
    unnamed x5 -> x3, waiting for transfers between devices: 0.08 us -> 158 us
    pallas_call x0 -> x1, Pallas kernels: none -> 116 us  [run_layer(): pl.pallas_call(layer, out_shape=[jax.ShapeDtypeStruct((rows, TILE), SUM),...]
    reshape x7 -> x15, local copies, waits for them, and re-layouts: 63.4 us -> 3.4 us  [the longest x3 1.17 us: run_layer(): ffn_bias = vectors[8:12].reshape(TILE, 4).T.reshape(4, 1, TILE)]
    while x31 -> x0, local copies, waits for them, and re-layouts: 43.5 us -> none  [the longest x2 20.3 us: local(): lax.map(attend_back, (qkv_blocks, key_blocks, log_total, grad_blocks))]
    unnamed x77 -> x19, local copies, waits for them, and re-layouts: 36.4 us -> 16.1 us
    reduce_sum x14 -> x6, other arithmetic: 21.6 us -> 4.02 us  [optimize(): jnp.sum(jnp.square(values[:, edges[index]:edges[index + 1]]))]
  transfers between devices with their start and end apart: 5 -> 2, of which waited for: 5 -> 2; matrix products, arithmetic and copies ran while one was open for 9% -> 1% of each run, Pallas kernels for 0% -> 0%
where the time goes in v1:
time: 475 us
  waiting for transfers between devices  262 us (55%)
  Pallas kernels  116 us (24%)
  blocking collectives  40.1 us (8%)
  local copies, waits for them, and re-layouts  21.7 us (5%)
  other arithmetic  20.3 us (4%)
  between operations  14.3 us (3%)
    unnamed x3, waiting for transfers between devices  158 us
    pallas_call x1, Pallas kernels, run_layer(): pl.pallas_call(layer, out_shape=[jax.ShapeDtypeStruct((rows, TILE), SUM),...  116 us
    all_gather x1, waiting for transfers between devices, fused(): walls = lax.all_gather(low, axes, axis=1, tiled=True)  104 us
    psum x1, blocking collectives, optimize(): norm_pairs = jnp.sqrt(lax.psum(squares, ('dp', 'shard')))  40.1 us
    unnamed x19, local copies, waits for them, and re-layouts  16.1 us
  transfers between devices with their start and end apart: 2, of which 2 were waited for; matrix products, arithmetic and copies ran while one was open for 1% of the time, Pallas kernels for 0%

profile of v1, /device:TPU:0, one launch (start us, length us, event | category | flops | bytes accessed | tf_op | source)
XLA Modules:
  0.0 474.6 jit_solution(6370837785640984728)
XLA Ops:
  7.3 1.2 convert_element_type.6
  8.5 0.4 copy.47
  8.9 0.5 copy.48
  9.7 0.8 pad_maximum_fusion.1
  10.8 0.6 reshape.101.qkv_bias
  11.4 0.4 reshape.92
  11.9 0.6 reshape.93.ffn_bias
  12.6 0.5 compare_select_fusion.valid
  13.1 104.5 %all-gather.2.cloned.1.call-done.walls = bf16[12,768,768]{2,1,0:T(8,128)(2,1)} async-done(((bf16[12,24,768]{2,1,0:T(8,128)(2,1)}), bf16[12,768,768]{2,1,0:T(8,128)(2,1)}) %all-gather.2.cloned.1.call-update) | async-done | bytes 14155792 | tf_op jit(solution)/shard_map/all_gather | solution.py:657
  117.5 115.9 %shard_map.177 = (f32[1152,768]{1,0:T(8,128)}, f32[1152,768]{1,0:T(8,128)}, bf16[12,768,768]{2,1,0:T(8,128)(2,1)}, f32[16,768]{1,0:T(8,128)}) custom-call(s32[4]{0:T(128)} %compare_select_fusion.valid, f32[1152,768]{1,0:T(8,128)} %tokens.1, f32[1152,768]{1,0:T(8,128)} %cotangent.1, bf16[12,768,768]{2,1,0:T(8,128)(2,1)} %all-gather.2.cloned.1.call-done.walls, ...), custom_call_target="tpu_custom_call" | custom-call | flops 60000002048 | bytes 60000000 | tf_op jit(solution)/shard_map/pallas_call | solution.py:606
  233.4 12.9 %copy.63 = bf16[96,8,12,768]{3,1,2,0:T(8,128)(2,1)} copy(bf16[96,8,12,768]{3,1,0,2:T(8,128)(2,1)} %bitcast.53) | data formatting | bytes 28311552
  246.4 1.1 copy-done
  247.5 0.6 multiply_reduce_fusion.3
  248.2 0.7 multiply_reduce_fusion.2
  248.8 0.7 multiply_reduce_fusion.1
  249.5 157.8 %reduce-scatter.4.cloned.1.call-done = bf16[24,9216]{1,0:T(8,128)(2,1)} async-done(((bf16[768,9216]{1,0:T(8,128)(2,1)}), bf16[24,9216]{1,0:T(8,128)(2,1)}) %reduce-scatter.4.cloned.1.call-update) | async-done | bytes 442384
  407.3 1.3 reshape.100
  408.9 0.7 copy.54
  409.6 0.4 copy.56
  410.5 3.2 multiply_add_fusion.1
  413.7 0.7 fusion.3
  414.3 0.7 fusion.4
  415.0 0.7 fusion.2
  415.7 2.6 maximum_bitcast_fusion
  418.4 2.7 maximum_bitcast_fusion.2
  421.0 40.1 %all-reduce = (f32[4,2]{1,0:T(4,128)S(1)}, f32[16,768]{1,0:T(8,128)S(1)}) all-reduce(f32[4,2]{1,0:T(4,128)S(1)} %pad_maximum_fusion.4, f32[16,768]{1,0:T(8,128)S(1)} %copy-done.3), channel_id=1, replica_groups=mesh['dp'=8,'shard'=4] {'dp','shard'}, use_global_device_ids=true, to_apply=%region_9.10 | all-reduce | flops 12296 | bytes 98368 | tf_op jit(solution)/shard_map/psum | solution.py:688
  461.1 0.7 fusion.6
  461.8 0.6 copy.58
  462.9 0.5 fusion.11
  463.4 2.6 select_multiply_fusion
  466.0 1.0 multiply_subtract_fusion
  467.1 0.7 divide_subtract_fusion
  (48 shorter events, 1.8 us)
Async XLA Ops:
  7.2 3.5 copy-start.1
  7.2 4.2 slice-start
  7.2 5.4 %copy-start.6 = (s32[4]{0:T(128)S(1)}, s32[4]{0:T(128)}, u32[]{:S(2)}) copy-start(s32[4]{0:T(128)} %param.12) | copy-start | bytes 52
  7.2 5.3 %copy-start.7 = (s32[4]{0:T(128)S(1)}, s32[4]{0:T(128)}, u32[]{:S(2)}) copy-start(s32[4]{0:T(128)} %param.13) | copy-start | bytes 52
  7.2 110.3 %all-gather.2.cloned.1.call-start = ((), (), s32[]{:S(2)}) async-start(), calls=%async_computation.1 | async-start | bytes 14598144 | tf_op jit(solution)/shard_map/all_gather | solution.py:657
  10.5 396.8 %reduce-scatter.4.cloned.1.call-start = ((), (), s32[]{:S(2)}) async-start(), calls=%async_computation.2 | async-start | bytes 14598144
  246.3 1.2 copy-start
  410.5 10.6 %copy-start.3 = (f32[16,768]{1,0:T(8,128)S(1)}, f32[16,768]{1,0:T(8,128)}, u32[]{:S(2)}) copy-start(f32[16,768]{1,0:T(8,128)} %get-tuple-element.17) | copy-start | bytes 147460
  413.7 53.4 %copy-start.2 = (f32[12,768]{1,0:T(8,128)S(1)}, f32[12,768]{1,0:T(8,128)}, u32[]{:S(2)}) copy-start(f32[12,768]{1,0:T(8,128)} %vectors.1) | copy-start | bytes 110596
  413.7 53.4 %copy-start.4 = (f32[12,768]{1,0:T(8,128)S(1)}, f32[12,768]{1,0:T(8,128)}, u32[]{:S(2)}) copy-start(f32[12,768]{1,0:T(8,128)} %param.19) | copy-start | bytes 110596
  413.7 53.4 %copy-start.5 = (f32[12,768]{1,0:T(8,128)S(1)}, f32[12,768]{1,0:T(8,128)}, u32[]{:S(2)}) copy-start(f32[12,768]{1,0:T(8,128)} %param.18) | copy-start | bytes 110596
Sparse Core Ops, SparseCore 0:
  11.6 105.9 all-gather.1
  246.5 160.7 reduce-scatter.3

commit v2 on v1

--- a/solution.py
+++ b/solution.py
@@ -357,7 +357,6 @@
 
 def attend_back(unit, slot, valid, qkv, grad_context, log_total, vec_grad):
     rows = slot_rows(slot)
-    items = []
     for half in range(2):
         query, key, value = (
             qkv[unit, rows, (3 * half + part) * 128 : (3 * half + part + 1) * 128]
@@ -368,57 +367,177 @@
         queries, keys, low_head = head_operands(query, key, valid)
         zero = jnp.zeros_like(grad)
         grads = (jnp.where(low_head, grad, zero), jnp.where(low_head, zero, grad))
-        items += [
-            (queries[head], keys[head], grads[head], query, key, value, grad) for head in range(2)
-        ]
-    scores = [dot(item[1], item[0], 1, 1) for item in items]
-    grad_probs = [dot(item[5], item[2], 1, 1) for item in items]
-    probs, grad_value = [], []
-    for index, item in enumerate(items):
-        probs.append(jnp.exp(scores[index] - log_total[unit, slot, index : index + 1, :]))
-        grad_value.append(dot(probs[index].astype(LOW), item[6], 1, 0))
-    grad_key, grad_query = [], []
-    for index, item in enumerate(items):
-        inner = sum_rows(grad_probs[index] * probs[index])
-        low = (probs[index] * (grad_probs[index] - inner)).astype(LOW)
-        grad_key.append(dot(low, item[3], 1, 0))
-        grad_query.append(dot(low, item[4], 0, 0))
-    for half in range(2):
-        first, second = 2 * half, 2 * half + 1
-        lanes = pl.ds(pl.multiple_of((unit + 3 * half) * 128, 128), 128)
+        scores = [dot(keys[head], queries[head], 1, 1) for head in range(2)]
+        grad_probs = [dot(value, grads[head], 1, 1) for head in range(2)]
+        probs, grad_value = [], []
+        for head in range(2):
+            index = 2 * half + head
+            probs.append(jnp.exp(scores[head] - log_total[unit, slot, index : index + 1, :]))
+            grad_value.append(dot(probs[head].astype(LOW), grad, 1, 0))
+        grad_key, grad_query = [], []
+        for head in range(2):
+            inner = sum_rows(grad_probs[head] * probs[head])
+            low = (probs[head] * (grad_probs[head] - inner)).astype(LOW)
+            grad_key.append(dot(low, query, 1, 0))
+            grad_query.append(dot(low, key, 0, 0))
         for part, parts, scale in (
             (0, grad_query, 0.125),
             (1, grad_key, 0.125),
             (2, grad_value, 1.0),
         ):
-            joined = (jnp.where(low_head, parts[first], parts[second]) * scale).astype(LOW)
+            joined = (jnp.where(low_head, parts[0], parts[1]) * scale).astype(LOW)
             qkv[unit, rows, (3 * half + part) * 128 : (3 * half + part + 1) * 128] = joined
             if part != 1:
                 row = part // 2
                 vec_grad[row : row + 1, lanes] += sum_rows(joined.astype(SUM))
 
 
+def place():
+    outer, inner = lax.axis_index("dp"), lax.axis_index("shard")
+    z, y, x, core = outer // 2, outer % 2, inner // 2, inner % 2
+    here = dict(z=z, y=y, x=x, core=core, high=z // 2, low=z % 2)
+    here["y1"], here["x1"] = y + core * (1 - 2 * y), x + (1 - core) * (1 - 2 * x)
+    here["y2"], here["x2"] = y + (1 - core) * (1 - 2 * y), x + core * (1 - 2 * x)
+    device = lambda z, y, x, core: (z * 2 + y, x * 2 + core)
+    here["twin"] = device(z, y, x, 1 - core)
+    here["near_z"] = device(z + 1 - 2 * (z % 2), y, x, core)
+    here["far_z"] = device((z + 2) % 4, y, x, core)
+    here["first"] = device(z, here["y1"], here["x1"], core)
+    here["second"] = device(z, here["y2"], here["x2"], core)
+    here["along_x"] = device(z, y, 1 - x, core)
+    here["along_y"] = device(z, 1 - y, x, core)
+    here["mine"] = pl.ds(pl.multiple_of(core * HALF, 128), HALF)
+    here["other"] = pl.ds(pl.multiple_of((1 - core) * HALF, 128), HALF)
+    return here
+
+
+def send(source, target, sent, arrived, device):
+    return pltpu.make_async_remote_copy(
+        src_ref=source,
+        dst_ref=target,
+        send_sem=sent,
+        recv_sem=arrived,
+        device_id=device,
+        device_id_type=pl.DeviceIdType.MESH,
+    )
+
+
+def inside(index):
+    if isinstance(index, int):
+        return 0 <= index < PIECES
+    return jnp.logical_and(index >= 0, index < PIECES)
+
+
+def guarded(index, body):
+    if isinstance(index, int):
+        if inside(index):
+            body(index)
+    else:
+        pl.when(inside(index))(lambda: body(index))
+
+
 def layer(
-    valid, tokens, cotangent, walls, vectors, qkv_bias, ffn_bias,
-    output, input_grad, pieces, vec_grad,
-    normed, token_low, qkv, context, hidden_low, act, slope, grad, grad_low, side, inverse,
-    log_total, mat, mat_low, in_sem, out_sem, mat_sem,
+    valid, tokens, cotangent, shard, vectors, qkv_bias, ffn_bias,
+    output, input_grad, grad_shard, vec_total,
+    walls, normed, token_low, qkv, context, hidden_low, act, slope, grad, grad_low, side, inverse,
+    log_total, vec_grad, mat, mat_send, mat_got, pair_keep, pair_send, pair_got,
+    line_keep, line_send, line_got, two_keep, two_send, two_got, one_keep, one_send, one_got, rows48,
+    shares, vec_got, in_sem, out_sem, twin_sem, gather_sent, gather_got, reduce_sent, reduce_got,
+    share_sem, vec_sent, vec_arrived,
 ):
-    def weight(piece):
-        return walls[piece]
+    here = place()
+    z, y, x, core, high, low = (here[name] for name in ("z", "y", "x", "core", "high", "low"))
+    y1, x1, y2, x2 = (here[name] for name in ("y1", "x1", "y2", "x2"))
+    mine, other = here["mine"], here["other"]
 
     cot_copy = pltpu.make_async_copy(cotangent, side, in_sem.at[0])
     cot_copy.start()
     tok_copy = pltpu.make_async_copy(tokens, normed, in_sem.at[1])
     tok_copy.start()
+
+    barrier = pltpu.get_barrier_semaphore()
+    peers = ("twin", "near_z", "far_z", "along_x", "along_y")
+    for name in peers:
+        pl.semaphore_signal(
+            barrier, inc=1, device_id=here[name], device_id_type=pl.DeviceIdType.MESH
+        )
+    pl.semaphore_wait(barrier, len(peers))
+
+    swap = send(
+        shard.at[:, :, other], shares.at[:, :, other], twin_sem.at[0], twin_sem.at[1], here["twin"]
+    )
+    swap.start()
+    vec_grad[...] = jnp.zeros_like(vec_grad)
+    swap.wait()
+
+    def fill(piece):
+        own, twin = shard[piece, :, mine], shares[piece, :, mine]
+        upper = jnp.where(core == 0, own, twin)
+        lower = jnp.where(core == 0, twin, own)
+        joined = jnp.concatenate([upper, lower], axis=0)
+        walls[piece, high, low, y, x, :, mine] = joined.astype(LOW)
+
+    each(PIECES, fill)
+
+    def gather_copy(piece, stage):
+        if stage == 0:
+            part, device = walls.at[piece, high, low, y, x, :, mine], here["far_z"]
+        elif stage == 1:
+            part, device = walls.at[piece, :, low, y, x, :, mine], here["near_z"]
+        elif stage == 2:
+            part, device = walls.at[piece, :, :, y, x, :, mine], here["first"]
+        elif stage == 3:
+            part, device = walls.at[piece, :, :, y, x, :, mine], here["second"]
+        elif stage == 4:
+            part, device = walls.at[piece, :, :, y1, x1, :, mine], here["second"]
+        else:
+            part, device = walls.at[piece, :, :, :, :, :, mine], here["twin"]
+        return send(part, part, gather_sent.at[piece, stage], gather_got.at[piece, stage], device)
+
+    def gather(notch):
+        def begin(piece):
+            gather_copy(piece, 0).start()
+
+        def spread_line(piece):
+            gather_copy(piece, 0).wait_recv()
+            gather_copy(piece, 1).start()
+
+        def spread_plane(piece):
+            gather_copy(piece, 1).wait_recv()
+            gather_copy(piece, 2).start()
+            gather_copy(piece, 3).start()
+
+        def pass_on(piece):
+            gather_copy(piece, 2).wait_recv()
+            gather_copy(piece, 4).start()
+
+        def share(piece):
+            gather_copy(piece, 3).wait_recv()
+            gather_copy(piece, 4).wait_recv()
+            gather_copy(piece, 5).start()
+
+        def finish(piece):
+            gather_copy(piece, 5).wait_recv()
+            for stage in range(6):
+                gather_copy(piece, stage).wait_send()
+
+        for age, body in enumerate((begin, spread_line, spread_plane, pass_on, share, finish)):
+            guarded(notch - age, body)
+
+    def weight(piece):
+        return walls[piece].reshape(TILE, TILE)
+
+    for notch in range(3):
+        gather(notch)
     tok_copy.wait()
-    vec_grad[...] = jnp.zeros_like(vec_grad)
 
     def cast_slot(slot):
         rows = slot_rows(slot)
         token_low[rows, :] = normed[rows, :].astype(LOW)
 
     each(4, cast_slot)
+    for notch in range(3, 6):
+        gather(notch)
 
     def project(unit):
         def project_slot(slot):
@@ -427,6 +546,7 @@
             qkv[unit, rows, :] = values.astype(LOW)
 
         each(4, project_slot)
+        gather(6 + unit)
         each(4, lambda slot: attend(unit, slot, valid[slot], qkv, context, log_total))
 
     each(3, project)
@@ -444,6 +564,8 @@
     each(4, attend_out)
 
     def widen(chunk):
+        gather(9 + chunk)
+
         def widen_slot(slot):
             rows = slot_rows(slot)
             pre = dot(hidden_low[rows, :], weight(4 + chunk), 1, 0) + ffn_bias[chunk]
@@ -457,13 +579,27 @@
     each(4, widen)
     cot_copy.wait()
 
-    def narrow(slot):
+    def clear_slot(slot):
         rows = slot_rows(slot)
-        ffn = dot(act[0, rows, :], weight(8), 1, 0)
-        for chunk in range(1, 4):
-            ffn += dot(act[chunk, rows, :], weight(8 + chunk), 1, 0)
-        hidden = normed[rows, :] * vectors[3:4, :] + vectors[4:5, :]
-        values = hidden + (ffn + vectors[5:6, :])
+        grad[rows, :] = normed[rows, :] * vectors[3:4, :] + (vectors[4:5, :] + vectors[5:6, :])
+
+    each(4, clear_slot)
+
+    def narrow(chunk):
+        gather(13 + chunk)
+
+        def narrow_slot(slot):
+            rows = slot_rows(slot)
+            grad[rows, :] += dot(act[chunk, rows, :], weight(8 + chunk), 1, 0)
+
+        each(4, narrow_slot)
+
+    each(3, narrow)
+    gather(16)
+
+    def finish_slot(slot):
+        rows = slot_rows(slot)
+        values = grad[rows, :] + dot(act[3, rows, :], weight(11), 1, 0)
         centred = values - mean_lanes(values)
         inv = lax.rsqrt(mean_lanes(centred * centred) + 1e-05)
         unit_values = centred * inv
@@ -478,47 +614,113 @@
             scaled - mean_lanes(scaled) - unit_values * mean_lanes(scaled * unit_values)
         )
         grad[rows, :] = result
-        low = result.astype(LOW)
-        grad_low[rows, :] = low
-        vec_grad[5:6, :] += sum_rows(low.astype(SUM))
-
-    each(4, narrow)
-
-    def piece_copy(index, piece):
-        slot = lax.rem(index, 2)
-        return pltpu.make_async_copy(mat_low.at[slot], pieces.at[piece], mat_sem.at[slot])
-
-    def emit(index, piece, left, right):
-        values = dot(left, right, 0, 0)
-
-        @pl.when(index >= 2)
-        def _():
-            piece_copy(index, piece).wait()
-
-        mat_low[lax.rem(index, 2)] = values.astype(LOW)
-        piece_copy(index, piece).start()
+        rounded = result.astype(LOW)
+        grad_low[rows, :] = rounded
+        vec_grad[5:6, :] += sum_rows(rounded.astype(SUM))
+
+    each(4, finish_slot)
+
+    def reduce_copy(index, stage):
+        turn = index % 2 if isinstance(index, int) else lax.rem(index, 2)
+        source, target, device = (
+            (mat_send, mat_got.at[turn], here["twin"]),
+            (pair_send, pair_got.at[turn], here["second"]),
+            (line_send, line_got.at[turn], here["first"]),
+            (two_send, two_got.at[turn], here["near_z"]),
+            (one_send, one_got.at[turn], here["far_z"]),
+        )[stage]
+        return send(source, target, reduce_sent.at[stage], reduce_got.at[stage, turn], device)
+
+    def share_copy(index):
+        part = shares.at[index, :, mine]
+        source = rows48.at[pl.ds(pl.multiple_of((1 - core) * 24, 8), 24), :]
+        return send(source, part, share_sem.at[0, index], share_sem.at[1, index], here["twin"])
+
+    def reduce(notch):
+        def turn_of(index):
+            return index % 2 if isinstance(index, int) else lax.rem(index, 2)
+
+        def shared(index):
+            share_copy(index).wait()
+
+        def last(index):
+            reduce_copy(index, 4).wait()
+            rows48[...] = one_keep[...] + one_got[turn_of(index)].astype(SUM)
+            shares[index, :, mine] = rows48[pl.ds(pl.multiple_of(core * 24, 8), 24), :]
+            share_copy(index).start()
+
+        def fourth(index):
+            reduce_copy(index, 3).wait()
+            turn = turn_of(index)
+            one_keep[...] = two_keep[high] + two_got[turn, high].astype(SUM)
+            one_send[...] = (two_keep[1 - high] + two_got[turn, 1 - high].astype(SUM)).astype(LOW)
+            reduce_copy(index, 4).start()
+
+        def third(index):
+            reduce_copy(index, 2).wait()
+            turn = turn_of(index)
+            two_send[...] = (
+                line_keep[:, 1 - low] + line_got[turn, :, 1 - low].astype(SUM)
+            ).astype(LOW)
+            reduce_copy(index, 3).start()
+            two_keep[...] = line_keep[:, low] + line_got[turn, :, low].astype(SUM)
+
+        def second(index):
+            reduce_copy(index, 1).wait()
+            turn = turn_of(index)
+            line_send[...] = (pair_keep[1] + pair_got[turn, 1].astype(SUM)).astype(LOW)
+            reduce_copy(index, 2).start()
+            line_keep[...] = pair_keep[0] + pair_got[turn, 0].astype(SUM)
+
+        def first(index):
+            reduce_copy(index, 0).wait()
+            turn = turn_of(index)
+
+            def column(row, col):
+                return mat[:, :, row, col, :, mine] + mat_got[turn, :, :, row, col].astype(SUM)
+
+            pair_send[0] = column(y2, x2).astype(LOW)
+            pair_send[1] = column(1 - y, 1 - x).astype(LOW)
+            reduce_copy(index, 1).start()
+            pair_keep[0] = column(y, x)
+            pair_keep[1] = column(y1, x1)
+
+        for age, body in ((6, shared), (5, last), (4, fourth), (3, third), (2, second), (1, first)):
+            guarded(notch - age, body)
+
+    def emit(index, left, right):
+        reduce(index)
+        for part in range(2):
+            values = dot(left[:, part * HALF : (part + 1) * HALF], right[...], 0, 0)
+            mat[part] = values.reshape(mat.shape[1:])
+        mat_send[...] = mat[:, :, :, :, :, other].astype(LOW)
+        reduce_copy(index, 0).start()
 
     def back_chunk(chunk):
-        emit(2 * chunk, 8 + chunk, act[chunk], grad_low[...])
+        emit(2 * chunk, act.at[chunk], grad_low)
 
         def back_slot(slot):
             rows = slot_rows(slot)
             values = dot(grad_low[rows, :], weight(8 + chunk), 1, 1)
-            low = (values * slope[chunk, rows, :].astype(SUM)).astype(LOW)
-            slope[chunk, rows, :] = low
+            rounded = (values * slope[chunk, rows, :].astype(SUM)).astype(LOW)
+            slope[chunk, rows, :] = rounded
             row = pl.ds(8 + chunk, 1)
-            vec_grad[row, :] += sum_rows(low.astype(SUM))
+            vec_grad[row, :] += sum_rows(rounded.astype(SUM))
 
         each(4, back_slot)
-        emit(2 * chunk + 1, 4 + chunk, hidden_low[...], slope[chunk])
+        emit(2 * chunk + 1, hidden_low, slope.at[chunk])
+
+        def back_hidden(slot):
+            rows = slot_rows(slot)
+            grad[rows, :] += dot(slope[chunk, rows, :], weight(4 + chunk), 1, 1)
+
+        each(4, back_hidden)
 
     each(4, back_chunk)
 
     def back_norm(slot):
         rows = slot_rows(slot)
         total = grad[rows, :]
-        for chunk in range(4):
-            total += dot(slope[chunk, rows, :], weight(4 + chunk), 1, 1)
         unit_values = normed[rows, :]
         vec_grad[3:4, :] += sum_rows(total * unit_values)
         vec_grad[4:5, :] += sum_rows(total)
@@ -528,12 +730,12 @@
             scaled - mean_lanes(scaled) - unit_values * mean_lanes(scaled * unit_values)
         )
         grad[rows, :] = result
-        low = result.astype(LOW)
-        grad_low[rows, :] = low
-        vec_grad[2:3, :] += sum_rows(low.astype(SUM))
+        rounded = result.astype(LOW)
+        grad_low[rows, :] = rounded
+        vec_grad[2:3, :] += sum_rows(rounded.astype(SUM))
 
     each(4, back_norm)
-    emit(8, 3, context[...], grad_low[...])
+    emit(8, context, grad_low)
 
     def back_context(slot):
         rows = slot_rows(slot)
@@ -546,9 +748,16 @@
             4,
             lambda slot: attend_back(unit, slot, valid[slot], qkv, context, log_total, vec_grad),
         )
-        emit(9 + unit, unit, token_low[...], qkv[unit])
+        emit(9 + unit, token_low, qkv.at[unit])
 
     each(3, back_unit)
+
+    order = ("twin", "along_x", "along_y", "near_z", "far_z")
+
+    def vec_copy(stage):
+        return send(
+            vec_grad, vec_got.at[stage], vec_sent.at[stage], vec_arrived.at[stage], here[order[stage]]
+        )
 
     def back_tokens(slot):
         rows = slot_rows(slot)
@@ -559,12 +768,22 @@
         side[rows, :] = total
         pltpu.make_async_copy(side.at[rows, :], input_grad.at[rows, :], out_sem.at[slot]).start()
 
-    each(4, back_tokens)
+    for step in range(6):
+        if step > 0:
+            vec_copy(step - 1).wait()
+            vec_grad[...] += vec_got[step - 1]
+        if step < 5:
+            vec_copy(step).start()
+        reduce(12 + step)
+        if step < 4:
+            back_tokens(step)
+    vec_total[...] = vec_grad[...]
+    out_copy = pltpu.make_async_copy(shares, grad_shard, in_sem.at[0])
+    out_copy.start()
+    out_copy.wait()
     for slot in range(4):
         rows = slot_rows(slot)
         pltpu.make_async_copy(side.at[rows, :], input_grad.at[rows, :], out_sem.at[slot]).wait()
-    piece_copy(10, 0).wait()
-    piece_copy(11, 0).wait()
 
 
 def permute_columns(shard):
@@ -592,7 +811,7 @@
     )
 
 
-def run_layer(tokens, cotangent, valid, walls, vectors):
+def run_layer(tokens, cotangent, valid, shard, vectors):
     rows = tokens.shape[0]
     zero = jnp.zeros((TILE,), SUM)
     qkv_bias = jnp.stack([vectors[0], zero, vectors[1]]).reshape(3, 2, 3, 128)
@@ -603,17 +822,19 @@
     hbm = pl.BlockSpec(memory_space=pl.ANY)
     full = lambda *shape: pltpu.VMEM(shape, SUM)
     low = lambda *shape: pltpu.VMEM(shape, LOW)
+    copies = lambda *shape: pltpu.SemaphoreType.DMA(shape)
     return pl.pallas_call(
         layer,
         out_shape=[
             jax.ShapeDtypeStruct((rows, TILE), SUM),
             jax.ShapeDtypeStruct((rows, TILE), SUM),
-            jax.ShapeDtypeStruct((PIECES, TILE, TILE), LOW),
+            jax.ShapeDtypeStruct((PIECES, 24, TILE), SUM),
             jax.ShapeDtypeStruct((16, TILE), SUM),
         ],
         in_specs=[smem, hbm, hbm, vmem, vmem, vmem, vmem],
         out_specs=[hbm, hbm, hbm, vmem],
         scratch_shapes=[
+            low(PIECES, 2, 2, 2, 2, 48, TILE),
             full(rows, TILE),
             low(rows, TILE),
             low(3, rows, TILE),
@@ -626,17 +847,43 @@
             full(rows, TILE),
             full(rows, 128),
             full(3, 4, 4, SLOT),
-            full(8, 128),
-            low(2, TILE, TILE),
-            pltpu.SemaphoreType.DMA((2,)),
-            pltpu.SemaphoreType.DMA((4,)),
-            pltpu.SemaphoreType.DMA((2,)),
+            full(16, TILE),
+            full(2, 2, 2, 2, 48, TILE),
+            low(2, 2, 2, 2, 48, HALF),
+            low(2, 2, 2, 2, 2, 48, HALF),
+            full(2, 2, 2, 48, HALF),
+            low(2, 2, 2, 48, HALF),
+            low(2, 2, 2, 2, 48, HALF),
+            full(2, 2, 48, HALF),
+            low(2, 2, 48, HALF),
+            low(2, 2, 2, 48, HALF),
+            full(2, 48, HALF),
+            low(2, 48, HALF),
+            low(2, 2, 48, HALF),
+            full(48, HALF),
+            low(48, HALF),
+            low(2, 48, HALF),
+            full(48, HALF),
+            full(PIECES, 24, TILE),
+            full(5, 16, TILE),
+            copies(2),
+            copies(4),
+            copies(2),
+            copies(PIECES, 6),
+            copies(PIECES, 6),
+            copies(5),
+            copies(5, 2),
+            copies(2, PIECES),
+            copies(5),
+            copies(5),
         ],
-        compiler_params=pltpu.CompilerParams(vmem_limit_bytes=63 * 2**20),
+        compiler_params=pltpu.CompilerParams(
+            collective_id=0, has_side_effects=True, vmem_limit_bytes=64 * 2**20
+        ),
         cost_estimate=pl.CostEstimate(
             flops=60 * 10**9, bytes_accessed=60 * 10**6, transcendentals=10**7
         ),
-    )(valid, tokens, cotangent, walls, vectors, qkv_bias, ffn_bias)
+    )(valid, tokens, cotangent, shard, vectors, qkv_bias, ffn_bias)
 
 
 def fused(
@@ -651,14 +898,13 @@
     vec_moment1,
     vec_moment2,
 ):
-    axes = ("dp", "shard")
     valid = jnp.where(null_flags == 1, QLEN, lengths).astype(jnp.int32)
-    low = permute_columns(weights.astype(LOW))
-    walls = lax.all_gather(low, axes, axis=1, tiled=True)
-    output, input_grad, pieces, vec_grad = run_layer(tokens, cotangent, valid, walls, vectors)
-    shard = lax.psum_scatter(pieces, axes, scatter_dimension=1, tiled=True)
-    grad_shard = restore_columns(shard.astype(SUM))
-    vec_total = lax.psum(vec_grad, axes)
+    shard = permute_columns(weights)
+    output, input_grad, grad_pieces, vec_total = run_layer(
+        tokens, cotangent, valid, shard, vectors
+    )
+    order = (9, 10, 11, 8, 1, 3, 5, 7, 0, 2, 4, 6)
+    grad_shard = restore_columns(jnp.stack([grad_pieces[index] for index in order]))
     ffn_rows = vec_total[8:12].T.reshape(4, TILE)
     vec_total = jnp.concatenate([vec_total[:8], ffn_rows], axis=0)
     return (output, input_grad) + optimize(

time: 475 us -> 276 us (0.58)
  waiting for transfers between devices: 262 us -> 0 us
  Pallas kernels: 116 us -> 199 us
  between operations: 14.3 us -> 0.85 us
  local copies, waits for them, and re-layouts: 21.7 us -> 14.6 us
    unnamed x3 -> x0, waiting for transfers between devices: 158 us -> none
    all_gather x1 -> x0, waiting for transfers between devices: 104 us -> none  [fused(): walls = lax.all_gather(low, axes, axis=1, tiled=True)]
    pallas_call x1, Pallas kernels: 116 us -> 199 us  [run_layer(): pl.pallas_call(layer, out_shape=[jax.ShapeDtypeStruct((rows, TILE), SUM),...]
    unnamed x19 -> x17, local copies, waits for them, and re-layouts: 16.1 us -> 6.64 us
  transfers between devices with their start and end apart: 2 -> 0, of which waited for: 2 -> 0; matrix products, arithmetic and copies ran while one was open for 1% -> 0% of each run, Pallas kernels for 0% -> 0%
where the time goes in v2:
time: 276 us; the launch traced here: 275 us
  Pallas kernels  199 us (72%)
  blocking collectives  37.6 us (14%)
  other arithmetic  22.6 us (8%)
  local copies, waits for them, and re-layouts  14.6 us (5%)
    pallas_call x1, Pallas kernels, run_layer(): pl.pallas_call(layer, out_shape=[jax.ShapeDtypeStruct((rows, TILE), SUM),...  199 us
    psum x1, blocking collectives, optimize(): norm_pairs = jnp.sqrt(lax.psum(squares, ('dp', 'shard')))  37.6 us
    reduce_sum x6, other arithmetic, optimize(): jnp.sum(jnp.square(values[:, edges[index]:edges[index + 1]]))  6.79 us
    unnamed x17, local copies, waits for them, and re-layouts  6.64 us

profile of v2, /device:TPU:0, one launch (start us, length us, event | category | flops | bytes accessed | tf_op | source)
XLA Modules:
  0.0 275.1 jit_solution(2227264689929783350)
XLA Ops:
  0.6 1.2 compare_select_fusion.valid
  1.8 1.7 multiply_reduce_fusion.1
  3.6 0.5 copy.47
  4.1 0.6 copy.48
  4.7 1.5 multiply_reduce_fusion.3
  6.2 1.6 multiply_reduce_fusion.2
  8.1 1.0 pad_maximum_fusion.shard
  9.3 0.6 reshape.99.qkv_bias
  9.9 0.4 reshape.92
  10.5 0.6 reshape.93.ffn_bias
  11.1 199.4 %shard_map.177 = (f32[1152,768]{1,0:T(8,128)}, f32[1152,768]{1,0:T(8,128)}, f32[12,24,768]{2,1,0:T(8,128)}, f32[16,768]{1,0:T(8,128)}) custom-call(s32[4]{0:T(128)} %compare_select_fusion.valid, f32[1152,768]{1,0:T(8,128)} %tokens.1, f32[1152,768]{1,0:T(8,128)} %cotangent.1, f32[12,24,768]{2,1,0:T(8,128)} %pad_maximum_fusion.shard, f32[12,768]{1,0:T(8,128)} %vectors.1, ...), custom_call_target="tpu_custom_call" | custom-call | flops 60000002048 | bytes 60000000 | tf_op jit(solution)/shard_map/pallas_call | solution.py:826
  210.5 1.2 slice_bitcast_fusion
  211.9 0.7 copy.54
  212.6 0.4 copy.56
  213.0 1.0 slice.110
  214.4 3.2 %multiply_add_fusion.1 = (f32[24,9216]{1,0:T(8,128)S(1)}, f32[24,9216]{1,0:T(8,128)}, f32[24,9216]{1,0:T(8,128)}) fusion(f32[24,9216]{1,0:T(8,128)S(1)} %copy-done, f32[24,3072]{1,0:T(8,128)S(1)} %bitcast.49, f32[24,3072]{1,0:T(8,128)S(1)} %copy.56, f32[24,768]{1,0:T(8,128)S(1)} %get-tuple-element.66, f32[24,2304]{1,0:T(8,128)S(1)} %reshape.95, ...), kind=kLoop, calls=%fused_computation.6 | loop fusion | flops 3317760 | bytes 6193152 | tf_op jit(solution)/shard_map/add | solution.py:921
  217.6 0.7 fusion.2
  218.3 2.7 maximum_bitcast_fusion.4
  221.0 0.7 fusion.3
  221.6 0.6 fusion.4
  222.2 2.7 maximum_bitcast_fusion.2
  224.9 37.6 %psum.7 = f32[4,2]{1,0:T(4,128)S(1)} all-reduce(f32[4,2]{1,0:T(4,128)S(1)} %pad_maximum_fusion.4), channel_id=1, replica_groups=mesh['dp'=8,'shard'=4] {'dp','shard'}, use_global_device_ids=true, to_apply=%region_8.9 | all-reduce | flops 8 | bytes 64 | tf_op jit(solution)/shard_map/psum | solution.py:934
  262.5 0.7 fusion.6
  263.2 0.5 fusion.10
  263.7 2.6 select_multiply_fusion
  266.3 1.0 multiply_subtract_fusion
  267.4 0.2 copy.57
  267.6 0.2 reshape.98
  267.8 0.7 divide_subtract_fusion
  268.5 0.6 copy.58
  269.1 4.2 %copy.65 = f32[1152,768]{1,0:T(8,128)} copy(f32[1152,768]{1,0:T(8,128)} %get-tuple-element.95) | data formatting | bytes 7077888
  273.3 1.8 copy.66
  (36 shorter events, 1.2 us)
Async XLA Ops:
  3.6 5.5 %copy-start.2 = (f32[12,768]{1,0:T(8,128)S(1)}, f32[12,768]{1,0:T(8,128)}, u32[]{:S(2)}) copy-start(f32[12,768]{1,0:T(8,128)} %vectors.1) | copy-start | bytes 110596
  3.6 6.3 %slice-start = ((f32[12,768]{1,0:T(8,128)}), f32[4,768]{1,0:T(4,128)S(1)}, s32[]{:S(2)}) async-start(f32[12,768]{1,0:T(8,128)} %vectors.1), calls=%async_computation | async-start | bytes 24576 | tf_op jit(solution)/shard_map/slice | solution.py:819
  211.8 2.6 copy-start
  214.4 53.0 %copy-start.6 = (f32[16,768]{1,0:T(8,128)S(1)}, f32[16,768]{1,0:T(8,128)}, u32[]{:S(2)}) copy-start(f32[16,768]{1,0:T(8,128)} %get-tuple-element.17) | copy-start | bytes 147460
  217.6 50.2 %copy-start.3 = (f32[12,768]{1,0:T(8,128)S(1)}, f32[12,768]{1,0:T(8,128)}, u32[]{:S(2)}) copy-start(f32[12,768]{1,0:T(8,128)} %vectors.1) | copy-start | bytes 110596
  217.6 50.2 %copy-start.4 = (f32[12,768]{1,0:T(8,128)S(1)}, f32[12,768]{1,0:T(8,128)}, u32[]{:S(2)}) copy-start(f32[12,768]{1,0:T(8,128)} %param.19) | copy-start | bytes 110596
  217.6 50.2 %copy-start.5 = (f32[12,768]{1,0:T(8,128)S(1)}, f32[12,768]{1,0:T(8,128)}, u32[]{:S(2)}) copy-start(f32[12,768]{1,0:T(8,128)} %param.18) | copy-start | bytes 110596
  269.1 4.2 %copy-start.1 = (f32[1152,768]{1,0:T(8,128)S(1)}, f32[1152,768]{1,0:T(8,128)}, u32[]{:S(2)}) copy-start(f32[1152,768]{1,0:T(8,128)} %get-tuple-element.96) | copy-start | bytes 10616836

commit v3 on v2

--- a/solution.py
+++ b/solution.py
@@ -284,6 +284,7 @@
 TILE = 768
 HALF = 384
 NEG = -1e9
+CORRECTION = 1.0 - 0.5**STEP
 
 
 def dot(left, right, left_dim, right_dim):
@@ -392,6 +393,22 @@
                 vec_grad[row : row + 1, lanes] += sum_rows(joined.astype(SUM))
 
 
+def make_order(buffer):
+    row = lax.broadcasted_iota(jnp.int32, (512, 512), 0)
+    column = lax.broadcasted_iota(jnp.int32, (512, 512), 1)
+    chosen = column == 4 * (row % 128) + row // 128
+    buffer[0, 0:512, 0:512] = jnp.where(chosen, 1.0, 0.0).astype(LOW)
+
+
+def reorder(values, buffer, side):
+    first = values.astype(LOW)
+    rest = values - first.astype(SUM)
+    second = rest.astype(LOW)
+    third = (rest - second.astype(SUM)).astype(LOW)
+    order = buffer[0, 0:512, 0:512]
+    return (dot(first, order, 1, side) + dot(second, order, 1, side)) + dot(third, order, 1, side)
+
+
 def place():
     outer, inner = lax.axis_index("dp"), lax.axis_index("shard")
     z, y, x, core = outer // 2, outer % 2, inner // 2, inner % 2
@@ -437,19 +454,44 @@
 
 
 def layer(
-    valid, tokens, cotangent, shard, vectors, qkv_bias, ffn_bias,
-    output, input_grad, grad_shard, vec_total,
+    lengths, null_flags, tokens, cotangent, weights, moment1, moment2, vectors, vec_moment1,
+    vec_moment2,
+    output, input_grad, new_moment1, new_moment2, new_weights, new_vec_moment1, new_vec_moment2,
+    new_vectors, norm_pairs, trust,
     walls, normed, token_low, qkv, context, hidden_low, act, slope, grad, grad_low, side, inverse,
     log_total, vec_grad, mat, mat_send, mat_got, pair_keep, pair_send, pair_got,
     line_keep, line_send, line_got, two_keep, two_send, two_got, one_keep, one_send, one_got, rows48,
-    shares, vec_got, in_sem, out_sem, twin_sem, gather_sent, gather_got, reduce_sent, reduce_got,
-    share_sem, vec_sent, vec_arrived,
+    shares, vec_got, qkv_bias, ffn_bias, squares, squares_got,
+    in_sem, out_sem, twin_sem, gather_sent, gather_got, reduce_sent, reduce_got,
+    share_sem, vec_sent, vec_arrived, state_sem, square_sem,
 ):
     here = place()
     z, y, x, core, high, low = (here[name] for name in ("z", "y", "x", "core", "high", "low"))
     y1, x1, y2, x2 = (here[name] for name in ("y1", "x1", "y2", "x2"))
     mine, other = here["mine"], here["other"]
 
+    def valid(slot):
+        return jnp.where(null_flags[slot] == 1, QLEN, lengths[slot])
+
+    def state_rows(quarter, chunk):
+        return pl.ds(quarter * SLOT + 24 * chunk, 24)
+
+    def state_copy(array, buffer, quarter, chunk):
+        return pltpu.make_async_copy(
+            array.at[:, pl.ds(TILE * chunk, TILE)],
+            buffer.at[state_rows(quarter, chunk), :],
+            state_sem.at[quarter, chunk],
+        )
+
+    def result_copy(array, quarter, chunk):
+        return pltpu.make_async_copy(
+            normed.at[state_rows(quarter, chunk), :],
+            array.at[:, pl.ds(TILE * chunk, TILE)],
+            state_sem.at[quarter, chunk],
+        )
+
+    for chunk in range(PIECES):
+        state_copy(weights, grad, 0, chunk).start()
     cot_copy = pltpu.make_async_copy(cotangent, side, in_sem.at[0])
     cot_copy.start()
     tok_copy = pltpu.make_async_copy(tokens, normed, in_sem.at[1])
@@ -463,21 +505,76 @@
         )
     pl.semaphore_wait(barrier, len(peers))
 
-    swap = send(
-        shard.at[:, :, other], shares.at[:, :, other], twin_sem.at[0], twin_sem.at[1], here["twin"]
-    )
-    swap.start()
+    for chunk in range(PIECES):
+        state_copy(weights, grad, 0, chunk).wait()
+    for unit in range(3):
+        for half in range(2):
+            for part in range(3):
+                lanes = slice((unit + 3 * half) * 128, (unit + 3 * half + 1) * 128)
+                place_lanes = slice((3 * half + part) * 128, (3 * half + part + 1) * 128)
+                grad[state_rows(1, unit), place_lanes] = grad[state_rows(0, part), lanes]
+
+    def swap(first, count):
+        rows = pl.ds(24 * first, 24 * count)
+        return send(
+            grad.at[pl.ds(SLOT + 24 * first, 24 * count), other],
+            shares.at[rows, other],
+            twin_sem.at[0, first],
+            twin_sem.at[1, first],
+            here["twin"],
+        )
+
+    swap(0, 3).start()
+    make_order(act)
+    for block in range(6):
+        values = jnp.concatenate(
+            [
+                grad[state_rows(0, 4 + part // 3), part % 3 * 256 : part % 3 * 256 + 256]
+                for part in (2 * block, 2 * block + 1)
+            ],
+            axis=1,
+        )
+        ordered = dot(values.astype(LOW), act[0, 0:512, 0:512], 1, 1)
+        for chunk in range(4):
+            grad[state_rows(1, 4 + chunk), block * 128 : block * 128 + 128] = ordered[
+                :, chunk * 128 : chunk * 128 + 128
+            ]
+    for chunk in (3, 8, 9, 10, 11):
+        grad[state_rows(1, chunk), :] = grad[state_rows(0, chunk), :]
+    swap(3, 9).start()
     vec_grad[...] = jnp.zeros_like(vec_grad)
-    swap.wait()
+    for unit in range(3):
+        for half in range(2):
+            lanes = slice((unit + 3 * half) * 128, (unit + 3 * half + 1) * 128)
+            for part, row in ((0, 0), (2, 1)):
+                target = slice((3 * half + part) * 128, (3 * half + part + 1) * 128)
+                qkv_bias[unit, :, target] = vectors[row : row + 1, lanes]
+            target = slice((3 * half + 1) * 128, (3 * half + 2) * 128)
+            qkv_bias[unit, :, target] = jnp.zeros((1, 128), SUM)
+    for block in range(6):
+        values = jnp.concatenate(
+            [
+                vectors[8 + part // 3 : 9 + part // 3, part % 3 * 256 : part % 3 * 256 + 256]
+                for part in (2 * block, 2 * block + 1)
+            ],
+            axis=1,
+        )
+        ordered = reorder(values, act, 1)
+        for chunk in range(4):
+            ffn_bias[chunk, :, block * 128 : block * 128 + 128] = ordered[
+                :, chunk * 128 : chunk * 128 + 128
+            ]
 
     def fill(piece):
-        own, twin = shard[piece, :, mine], shares[piece, :, mine]
+        rows = pl.ds(pl.multiple_of(24 * piece, 8), 24)
+        own, twin = grad[pl.ds(pl.multiple_of(SLOT + 24 * piece, 8), 24), mine], shares[rows, mine]
         upper = jnp.where(core == 0, own, twin)
         lower = jnp.where(core == 0, twin, own)
         joined = jnp.concatenate([upper, lower], axis=0)
         walls[piece, high, low, y, x, :, mine] = joined.astype(LOW)
 
-    each(PIECES, fill)
+    swap(0, 3).wait()
+    each(3, fill)
 
     def gather_copy(piece, stage):
         if stage == 0:
@@ -527,8 +624,11 @@
     def weight(piece):
         return walls[piece].reshape(TILE, TILE)
 
-    for notch in range(3):
-        gather(notch)
+    gather(0)
+    swap(3, 9).wait()
+    each(9, lambda piece: fill(3 + piece))
+    gather(1)
+    gather(2)
     tok_copy.wait()
 
     def cast_slot(slot):
@@ -547,7 +647,7 @@
 
         each(4, project_slot)
         gather(6 + unit)
-        each(4, lambda slot: attend(unit, slot, valid[slot], qkv, context, log_total))
+        each(4, lambda slot: attend(unit, slot, valid(slot), qkv, context, log_total))
 
     each(3, project)
 
@@ -579,22 +679,24 @@
     each(4, widen)
     cot_copy.wait()
 
-    def clear_slot(slot):
+    def narrow_first(slot):
         rows = slot_rows(slot)
-        grad[rows, :] = normed[rows, :] * vectors[3:4, :] + (vectors[4:5, :] + vectors[5:6, :])
-
-    each(4, clear_slot)
+        start = normed[rows, :] * vectors[3:4, :] + (vectors[4:5, :] + vectors[5:6, :])
+        grad[rows, :] = start + dot(act[0, rows, :], weight(8), 1, 0)
+
+    gather(13)
+    each(4, narrow_first)
 
     def narrow(chunk):
-        gather(13 + chunk)
+        gather(14 + chunk)
 
         def narrow_slot(slot):
             rows = slot_rows(slot)
-            grad[rows, :] += dot(act[chunk, rows, :], weight(8 + chunk), 1, 0)
+            grad[rows, :] += dot(act[1 + chunk, rows, :], weight(9 + chunk), 1, 0)
 
         each(4, narrow_slot)
 
-    each(3, narrow)
+    each(2, narrow)
     gather(16)
 
     def finish_slot(slot):
@@ -603,7 +705,7 @@
         centred = values - mean_lanes(values)
         inv = lax.rsqrt(mean_lanes(centred * centred) + 1e-05)
         unit_values = centred * inv
-        kept = lax.broadcasted_iota(jnp.int32, (SLOT, 1), 0) < valid[slot]
+        kept = lax.broadcasted_iota(jnp.int32, (SLOT, 1), 0) < valid(slot)
         grad_out = jnp.where(kept, side[rows, :], 0.0)
         side[rows, :] = unit_values * vectors[6:7, :] + vectors[7:8, :]
         pltpu.make_async_copy(side.at[rows, :], output.at[rows, :], out_sem.at[slot]).start()
@@ -632,7 +734,7 @@
         return send(source, target, reduce_sent.at[stage], reduce_got.at[stage, turn], device)
 
     def share_copy(index):
-        part = shares.at[index, :, mine]
+        part = shares.at[pl.ds(pl.multiple_of(24 * index, 8), 24), mine]
         source = rows48.at[pl.ds(pl.multiple_of((1 - core) * 24, 8), 24), :]
         return send(source, part, share_sem.at[0, index], share_sem.at[1, index], here["twin"])
 
@@ -646,7 +748,9 @@
         def last(index):
             reduce_copy(index, 4).wait()
             rows48[...] = one_keep[...] + one_got[turn_of(index)].astype(SUM)
-            shares[index, :, mine] = rows48[pl.ds(pl.multiple_of(core * 24, 8), 24), :]
+            shares[pl.ds(pl.multiple_of(24 * index, 8), 24), mine] = rows48[
+                pl.ds(pl.multiple_of(core * 24, 8), 24), :
+            ]
             share_copy(index).start()
 
         def fourth(index):
@@ -736,6 +840,10 @@
 
     each(4, back_norm)
     emit(8, context, grad_low)
+    states = (moment1, moment2, weights)
+    for quarter, array in enumerate(states):
+        for chunk in range(PIECES):
+            state_copy(array, normed, quarter, chunk).start()
 
     def back_context(slot):
         rows = slot_rows(slot)
@@ -746,7 +854,7 @@
     def back_unit(unit):
         each(
             4,
-            lambda slot: attend_back(unit, slot, valid[slot], qkv, context, log_total, vec_grad),
+            lambda slot: attend_back(unit, slot, valid(slot), qkv, context, log_total, vec_grad),
         )
         emit(9 + unit, token_low, qkv.at[unit])
 
@@ -767,6 +875,108 @@
             total += dot(qkv[unit, rows, :], weight(unit), 1, 1)
         side[rows, :] = total
         pltpu.make_async_copy(side.at[rows, :], input_grad.at[rows, :], out_sem.at[slot]).start()
+
+    def adapt(first, second, value, held):
+        new_first = 0.5 * first + 0.5 * value
+        new_second = 0.5 * second + 0.5 * value * value
+        step = (new_first / CORRECTION) / (jnp.sqrt(new_second / CORRECTION) + 1e-06)
+        if held is not None:
+            step = step + 0.01 * held
+        return new_first, new_second, step
+
+    def lane_sums(values):
+        total = sum_rows(values)
+        return sum(total[:, 128 * index : 128 * index + 128] for index in range(6))
+
+    def group_of(chunk):
+        return 0 if chunk < 3 else 1 if chunk == 3 else 2 if chunk < 8 else 3
+
+    def adapt_chunk(chunk):
+        row = 4 + group_of(chunk)
+        first, second, step = adapt(
+            *(normed[state_rows(quarter, chunk), :] for quarter in (0, 1, 3, 2))
+        )
+        normed[state_rows(0, chunk), :] = first
+        normed[state_rows(1, chunk), :] = second
+        normed[state_rows(3, chunk), :] = step
+        result_copy(new_moment1, 0, chunk).start()
+        result_copy(new_moment2, 1, chunk).start()
+        squares[row : row + 1, :] += lane_sums(step * step)
+
+    def weight_squares():
+        squares[...] = jnp.zeros_like(squares)
+        for quarter, array in enumerate(states):
+            for chunk in range(PIECES):
+                state_copy(array, normed, quarter, chunk).wait()
+        for chunk in range(PIECES):
+            held = normed[state_rows(2, chunk), :]
+            row = group_of(chunk)
+            squares[row : row + 1, :] += lane_sums(held * held)
+
+    def adapt_early():
+        make_order(act)
+        normed[state_rows(3, 3), :] = shares[pl.ds(24 * 8, 24), :]
+        for chunk in range(4):
+            normed[state_rows(3, 8 + chunk), :] = shares[pl.ds(24 * 2 * chunk, 24), :]
+        for block in range(6):
+            values = jnp.concatenate(
+                [
+                    shares[pl.ds(24 * (2 * chunk + 1), 24), block * 128 : block * 128 + 128]
+                    for chunk in range(4)
+                ],
+                axis=1,
+            )
+            ordered = reorder(values, act, 0)
+            for half in range(2):
+                part = 2 * block + half
+                lanes = slice(part % 3 * 256, part % 3 * 256 + 256)
+                normed[state_rows(3, 4 + part // 3), lanes] = ordered[
+                    :, half * 256 : half * 256 + 256
+                ]
+        for chunk in range(3, PIECES):
+            adapt_chunk(chunk)
+
+    def adapt_late():
+        for unit in range(3):
+            for half in range(2):
+                for part in range(3):
+                    lanes = slice((unit + 3 * half) * 128, (unit + 3 * half + 1) * 128)
+                    source = slice((3 * half + part) * 128, (3 * half + part + 1) * 128)
+                    normed[state_rows(3, part), lanes] = shares[pl.ds(24 * (9 + unit), 24), source]
+        for chunk in range(3):
+            adapt_chunk(chunk)
+
+    def adapt_vectors():
+        for block in range(6):
+            values = jnp.concatenate(
+                [
+                    vec_grad[8 + chunk : 9 + chunk, block * 128 : block * 128 + 128]
+                    for chunk in range(4)
+                ],
+                axis=1,
+            )
+            ordered = reorder(values, act, 0)
+            for half in range(2):
+                part = 2 * block + half
+                lanes = slice(part % 3 * 256, part % 3 * 256 + 256)
+                row = 8 + part // 3
+                vec_got[0, row : row + 1, lanes] = ordered[:, half * 256 : half * 256 + 256]
+        vec_got[0, 0:8, :] = vec_grad[0:8, :]
+        first, second, step = adapt(
+            vec_moment1[...], vec_moment2[...], vec_got[0, 0:12, :], None
+        )
+        new_vec_moment1[...] = first
+        new_vec_moment2[...] = second
+        new_vectors[...] = vectors[...] - 0.3 * step
+
+    def square_copy(stage):
+        return send(
+            squares,
+            squares_got.at[stage],
+            square_sem.at[0, stage],
+            square_sem.at[1, stage],
+            here[order[stage]],
+        )
 
     for step in range(6):
         if step > 0:
@@ -777,62 +987,73 @@
         reduce(12 + step)
         if step < 4:
             back_tokens(step)
-    vec_total[...] = vec_grad[...]
-    out_copy = pltpu.make_async_copy(shares, grad_shard, in_sem.at[0])
-    out_copy.start()
-    out_copy.wait()
+        if step == 0:
+            weight_squares()
+        if step == 3:
+            adapt_early()
+    adapt_late()
+    for stage in range(5):
+        square_copy(stage).start()
+        if stage == 0:
+            adapt_vectors()
+        square_copy(stage).wait()
+        squares[...] += squares_got[stage]
+    norms = jnp.sqrt(jnp.sum(squares[...], axis=1, keepdims=True))
+    ratio = norms[0:4] / (norms[4:8] + 1e-06)
+    norm_pairs[:, 0:1] = norms[0:4]
+    norm_pairs[:, 1:2] = norms[4:8]
+    for group in range(4):
+        trust[group] = ratio[group, 0]
+    for chunk in range(PIECES):
+        group = group_of(chunk)
+        rows = state_rows(2, chunk)
+        factor = 0.3 * ratio[group : group + 1, :]
+        normed[rows, :] = normed[rows, :] - factor * normed[state_rows(3, chunk), :]
+        result_copy(new_weights, 2, chunk).start()
+    for quarter, array in enumerate((new_moment1, new_moment2, new_weights)):
+        for chunk in range(PIECES):
+            result_copy(array, quarter, chunk).wait()
     for slot in range(4):
         rows = slot_rows(slot)
         pltpu.make_async_copy(side.at[rows, :], input_grad.at[rows, :], out_sem.at[slot]).wait()
 
 
-def permute_columns(shard):
-    rows = shard.shape[0]
-    first = shard[:, :2304].reshape(rows, 3, 2, 3, 128).transpose(3, 0, 2, 1, 4)
-    second = shard[:, 2304:3072].reshape(1, rows, TILE)
-    third = shard[:, 3072:6144].reshape(rows, TILE, 4).transpose(2, 0, 1)
-    fourth = shard[:, 6144:].reshape(rows, 4, TILE).transpose(1, 0, 2)
-    return jnp.concatenate([first.reshape(3, rows, TILE), second, third, fourth], axis=0)
-
-
-def restore_columns(pieces):
-    rows = pieces.shape[1]
-    first = pieces[:3].reshape(3, rows, 2, 3, 128).transpose(1, 3, 2, 0, 4)
-    third = pieces[4:8].transpose(1, 2, 0)
-    fourth = pieces[8:].transpose(1, 0, 2)
-    return jnp.concatenate(
-        [
-            first.reshape(rows, 2304),
-            pieces[3],
-            third.reshape(rows, 3072),
-            fourth.reshape(rows, 3072),
-        ],
-        axis=1,
-    )
-
-
-def run_layer(tokens, cotangent, valid, shard, vectors):
+def fused(
+    tokens,
+    cotangent,
+    lengths,
+    null_flags,
+    weights,
+    moment1,
+    moment2,
+    vectors,
+    vec_moment1,
+    vec_moment2,
+):
     rows = tokens.shape[0]
-    zero = jnp.zeros((TILE,), SUM)
-    qkv_bias = jnp.stack([vectors[0], zero, vectors[1]]).reshape(3, 2, 3, 128)
-    qkv_bias = qkv_bias.transpose(2, 1, 0, 3).reshape(3, 1, TILE)
-    ffn_bias = vectors[8:12].reshape(TILE, 4).T.reshape(4, 1, TILE)
     vmem = pl.BlockSpec(memory_space=pltpu.VMEM)
     smem = pl.BlockSpec(memory_space=pltpu.SMEM)
     hbm = pl.BlockSpec(memory_space=pl.ANY)
     full = lambda *shape: pltpu.VMEM(shape, SUM)
     low = lambda *shape: pltpu.VMEM(shape, LOW)
     copies = lambda *shape: pltpu.SemaphoreType.DMA(shape)
+    like = lambda array: jax.ShapeDtypeStruct(array.shape, array.dtype)
     return pl.pallas_call(
         layer,
         out_shape=[
-            jax.ShapeDtypeStruct((rows, TILE), SUM),
-            jax.ShapeDtypeStruct((rows, TILE), SUM),
-            jax.ShapeDtypeStruct((PIECES, 24, TILE), SUM),
-            jax.ShapeDtypeStruct((16, TILE), SUM),
+            like(tokens),
+            like(tokens),
+            like(weights),
+            like(weights),
+            like(weights),
+            like(vectors),
+            like(vectors),
+            like(vectors),
+            jax.ShapeDtypeStruct((4, 2), SUM),
+            jax.ShapeDtypeStruct((4,), SUM),
         ],
-        in_specs=[smem, hbm, hbm, vmem, vmem, vmem, vmem],
-        out_specs=[hbm, hbm, hbm, vmem],
+        in_specs=[smem, smem] + [hbm] * 5 + [vmem] * 3,
+        out_specs=[hbm] * 5 + [vmem] * 4 + [smem],
         scratch_shapes=[
             low(PIECES, 2, 2, 2, 2, 48, TILE),
             full(rows, TILE),
@@ -864,11 +1085,15 @@
             low(48, HALF),
             low(2, 48, HALF),
             full(48, HALF),
-            full(PIECES, 24, TILE),
+            full(SLOT, TILE),
             full(5, 16, TILE),
+            full(3, 1, TILE),
+            full(4, 1, TILE),
+            full(8, 128),
+            full(5, 8, 128),
             copies(2),
             copies(4),
-            copies(2),
+            copies(2, 4),
             copies(PIECES, 6),
             copies(PIECES, 6),
             copies(5),
@@ -876,6 +1101,8 @@
             copies(2, PIECES),
             copies(5),
             copies(5),
+            copies(3, PIECES),
+            copies(2, 5),
         ],
         compiler_params=pltpu.CompilerParams(
             collective_id=0, has_side_effects=True, vmem_limit_bytes=64 * 2**20
@@ -883,77 +1110,17 @@
         cost_estimate=pl.CostEstimate(
             flops=60 * 10**9, bytes_accessed=60 * 10**6, transcendentals=10**7
         ),
-    )(valid, tokens, cotangent, shard, vectors, qkv_bias, ffn_bias)
-
-
-def fused(
-    tokens,
-    cotangent,
-    lengths,
-    null_flags,
-    weights,
-    moment1,
-    moment2,
-    vectors,
-    vec_moment1,
-    vec_moment2,
-):
-    valid = jnp.where(null_flags == 1, QLEN, lengths).astype(jnp.int32)
-    shard = permute_columns(weights)
-    output, input_grad, grad_pieces, vec_total = run_layer(
-        tokens, cotangent, valid, shard, vectors
-    )
-    order = (9, 10, 11, 8, 1, 3, 5, 7, 0, 2, 4, 6)
-    grad_shard = restore_columns(jnp.stack([grad_pieces[index] for index in order]))
-    ffn_rows = vec_total[8:12].T.reshape(4, TILE)
-    vec_total = jnp.concatenate([vec_total[:8], ffn_rows], axis=0)
-    return (output, input_grad) + optimize(
-        grad_shard, vec_total, weights, moment1, moment2, vectors, vec_moment1, vec_moment2
-    )
-
-
-def optimize(
-    grad_shard, vec_total, weights, moment1, moment2, vectors, vec_moment1, vec_moment2
-):
-    correction = 1.0 - 0.5**STEP
-    new_first = 0.5 * moment1 + 0.5 * grad_shard
-    new_second = 0.5 * moment2 + 0.5 * grad_shard * grad_shard
-    update = new_first / correction / (jnp.sqrt(new_second / correction) + 1e-06) + 0.01 * weights
-    edges = (0, 2304, 3072, 6144, 9216)
-    squares = jnp.stack(
-        [
-            jnp.stack(
-                [
-                    jnp.sum(jnp.square(values[:, edges[index] : edges[index + 1]]))
-                    for values in (weights, update)
-                ]
-            )
-            for index in range(4)
-        ]
-    )
-    norm_pairs = jnp.sqrt(lax.psum(squares, ("dp", "shard")))
-    trust = norm_pairs[:, 0] / (norm_pairs[:, 1] + 1e-06)
-    column = jnp.arange(weights.shape[1])
-    column_trust = jnp.where(
-        column < edges[1],
-        trust[0],
-        jnp.where(column < edges[2], trust[1], jnp.where(column < edges[3], trust[2], trust[3])),
-    )
-    new_weights = weights - 0.3 * column_trust * update
-    vec_first = 0.5 * vec_moment1 + 0.5 * vec_total
-    vec_second = 0.5 * vec_moment2 + 0.5 * vec_total * vec_total
-    new_vectors = vectors - 0.3 * (vec_first / correction) / (
-        jnp.sqrt(vec_second / correction) + 1e-06
-    )
-    return (
-        new_first,
-        new_second,
-        new_weights,
-        vec_first,
-        vec_second,
-        new_vectors,
-        norm_pairs,
-        trust,
+    )(
+        lengths,
+        null_flags,
+        tokens,
+        cotangent,
+        weights,
+        moment1,
+        moment2,
+        vectors,
+        vec_moment1,
+        vec_moment2,
     )
 
 

time: 276 us -> 225 us (0.82)
  blocking collectives: 37.6 us -> 0 us
  other arithmetic: 22.6 us -> 0 us
  Pallas kernels: 199 us -> 212 us
    psum x1 -> x0, blocking collectives: 37.6 us -> none  [optimize(): norm_pairs = jnp.sqrt(lax.psum(squares, ('dp', 'shard')))]
    pallas_call x1, Pallas kernels: 199 us -> 212 us  [fused(): pl.pallas_call(layer, out_shape=[like(tokens), like(tokens), like(weights...]
    reduce_sum x6 -> x0, other arithmetic: 6.79 us -> none  [optimize(): jnp.sum(jnp.square(values[:, edges[index]:edges[index + 1]]))]
    another operation x4 -> x0, other arithmetic: 5.41 us -> none  [the longest x3 5.33 us: optimize(): jnp.stack([jnp.stack([jnp.sum(jnp.square(values[:, edges[index]:edges[ind...]
    unnamed x17 -> x25, local copies, waits for them, and re-layouts: 6.64 us -> 11.1 us
    reshape x14 -> x0, local copies, waits for them, and re-layouts: 3.6 us -> none  [the longest x3 1.17 us: run_layer(): ffn_bias = vectors[8:12].reshape(TILE, 4).T.reshape(4, 1, TILE)]
    add x1 -> x0, other arithmetic: 3.21 us -> none  [optimize(): new_first / correction / (jnp.sqrt(new_second / correction) + 1e-06)]
where the time goes in v3:
time: 225 us
  Pallas kernels  212 us (94%)
  local copies, waits for them, and re-layouts  12.4 us (6%)
    pallas_call x1, Pallas kernels, fused(): pl.pallas_call(layer, out_shape=[like(tokens), like(tokens), like(weights...  212 us
    unnamed x25, local copies, waits for them, and re-layouts  11.1 us

profile of v3, /device:TPU:0, one launch (start us, length us, event | category | flops | bytes accessed | tf_op | source)
XLA Modules:
  0.0 225.1 jit_solution(12991669249116699454)
XLA Ops:
  0.6 212.0 %shard_map.177 = (f32[1152,768]{1,0:T(8,128)}, f32[1152,768]{1,0:T(8,128)}, f32[24,9216]{1,0:T(8,128)}, f32[24,9216]{1,0:T(8,128)}, f32[24,9216]{1,0:T(8,128)}, ...) custom-call(s32[4]{0:T(128)} %lengths.1, s32[4]{0:T(128)} %null_flags.1, ...), custom_call_target="tpu_custom_call" | custom-call | flops 60000002048 | bytes 60000000 | tf_op jit(solution)/shard_map/pallas_call | solution.py:1041
  212.6 1.3 copy.20
  213.9 0.0 copy-start
  213.9 4.2 %copy.30 = f32[1152,768]{1,0:T(8,128)} copy(f32[1152,768]{1,0:T(8,128)} %get-tuple-element.30) | data formatting | bytes 7077888
  218.1 0.0 copy-done
  218.1 0.0 copy-start.3
  218.1 0.0 copy-start.2
  218.1 1.8 copy.31
  219.9 0.0 copy-done.3
  219.9 0.0 copy-start.1
  219.9 0.0 copy-start.6
  219.9 0.0 copy-start.5
  219.9 0.0 copy-start.4
  219.9 0.0 copy-start.7
  219.9 0.9 copy.32
  220.9 0.0 copy-done.2
  220.9 0.9 copy.33
  221.8 0.0 copy-done.1
  221.8 0.9 copy.34
  222.7 0.0 copy-done.6
  222.7 0.6 copy.35
  223.3 0.0 copy-done.5
  223.3 0.6 copy.36
  223.9 0.0 copy-done.4
  223.9 0.6 copy.37
  224.6 0.0 copy-done.7
  224.6 0.5 copy.38
Async XLA Ops:
  213.9 4.2 %copy-start = (f32[1152,768]{1,0:T(8,128)S(1)}, f32[1152,768]{1,0:T(8,128)}, u32[]{:S(2)}) copy-start(f32[1152,768]{1,0:T(8,128)} %get-tuple-element.31) | copy-start | bytes 10616836
  218.1 1.8 copy-start.3
  218.1 2.8 %copy-start.2 = (f32[24,9216]{1,0:T(8,128)S(1)}, f32[24,9216]{1,0:T(8,128)}, u32[]{:S(2)}) copy-start(f32[24,9216]{1,0:T(8,128)} %get-tuple-element.33) | copy-start | bytes 2654212
  219.9 1.9 copy-start.1
  219.9 2.8 %copy-start.6 = (f32[12,768]{1,0:T(8,128)S(1)}, f32[12,768]{1,0:T(8,128)}, u32[]{:S(2)}) copy-start(f32[12,768]{1,0:T(8,128)} %get-tuple-element.35) | copy-start | bytes 110596
  219.9 3.4 %copy-start.5 = (f32[12,768]{1,0:T(8,128)S(1)}, f32[12,768]{1,0:T(8,128)}, u32[]{:S(2)}) copy-start(f32[12,768]{1,0:T(8,128)} %get-tuple-element.36) | copy-start | bytes 110596
  219.9 4.0 %copy-start.4 = (f32[12,768]{1,0:T(8,128)S(1)}, f32[12,768]{1,0:T(8,128)}, u32[]{:S(2)}) copy-start(f32[12,768]{1,0:T(8,128)} %get-tuple-element.37) | copy-start | bytes 110596
  219.9 4.6 %copy-start.7 = (f32[4]{0:T(128)S(1)}, f32[4]{0:T(128)}, u32[]{:S(2)}) copy-start(f32[4]{0:T(128)} %get-tuple-element.39) | copy-start | bytes 52
